TPU v7x, 32 devices: a whole 2x2x4 slice. The times are simulated.
32 devices in a mesh: dp: 8 (over z, y), tensor: 4 (over x, core).
Axes of the slice: x: 2, y: 2, z: 4, core: 2. Of those that a mesh axis runs over, the one named last changes fastest.
Arguments:
- hidden_in: bfloat16 [8, 8, 256, 768], P(None, 'dp', 'tensor'), may hold values from -6 to 6
- lengths: int32 [8], replicated, may hold values from 1537 to 2048, as said below
- order: int32 [8], replicated, may hold values from 0 to 7, each once
- in_gain: float32 [2, 768], replicated, may hold values from 0.1 to 1.9
- w_z: bfloat16 [2, 768, 1536], P(None, 'dp', 'tensor'), may hold values from -0.21875 to 0.21875
- w_x: bfloat16 [2, 768, 1536], P(None, 'dp', 'tensor'), may hold values from -0.21875 to 0.21875
- w_bc: bfloat16 [2, 768, 256], P(None, 'dp'), may hold values from -0.21875 to 0.21875
- w_dt: bfloat16 [2, 768, 24], P(None, 'dp', 'tensor'), may hold values from -0.21875 to 0.21875
- conv_x: float32 [2, 5, 1536], replicated, may hold values from -3 to 3
- conv_bc: float32 [2, 5, 256], replicated, may hold values from -3 to 3
- dt_bias: float32 [2, 24], replicated, may hold values from -4 to -2
- a_log: float32 [2, 24], replicated, may hold values from -5.3 to 0
- d_skip: float32 [2, 24], replicated, may hold values from 0.5 to 1.5
- gated_gain: float32 [2, 1536], replicated, may hold values from 0.1 to 1.9
- w_out: bfloat16 [2, 768, 1536], P(None, 'dp', 'tensor'), may hold values from -0.15625 to 0.15625
- cotangent: bfloat16 [8, 8, 256, 768], P('dp', None, 'tensor'), may hold values from -6 to 6
Outputs:
- block_out: bfloat16 [8, 8, 256, 768], P('dp', None, 'tensor')
- input_grad: bfloat16 [8, 8, 256, 768], P(None, 'dp', 'tensor')
- grad_in_gain: float32 [2, 768], replicated
- grad_w_z: float32 [2, 768, 1536], P(None, 'dp', 'tensor')
- grad_w_x: float32 [2, 768, 1536], P(None, 'dp', 'tensor')
- grad_w_bc: float32 [2, 768, 256], P(None, 'dp')
- grad_w_dt: float32 [2, 768, 24], P(None, 'dp', 'tensor')
- grad_conv_x: float32 [2, 5, 1536], replicated
- grad_conv_bc: float32 [2, 5, 256], replicated
- grad_dt_bias: float32 [2, 24], replicated
- grad_a_log: float32 [2, 24], replicated
- grad_d_skip: float32 [2, 24], replicated
- grad_gated_gain: float32 [2, 1536], replicated
- grad_w_out: float32 [2, 768, 1536], P(None, 'dp', 'tensor')
Inputs may be any that keep to these rules, and one draw needn't show every extreme that they name: `lengths`: every length is over 1536 and one sequence has exactly 2048. `order`: each sequence number once.
All inputs are finite; a program needn't handle non-finite values.
Results may differ from a plain program's by a relative error of at most 0.03.
The roundings to bfloat16 on the way count: a program that leaves them out, or rounds other values in their place, can miss the bound.
Values may be sent and summed in bfloat16 or wider, within the bound.
A program may use at most 256 MiB of HBM per device.

v0:
```python
from functools import partial

import jax
import jax.numpy as jnp
from jax import lax
from jax.sharding import PartitionSpec as P

SCAN_BLOCK = 256


EPS = 1e-05
HIGH = lax.Precision.HIGHEST
CONTRACT_FIRST = (((0,), (0,)), ((), ()))


def rounded(values):
    return lax.optimization_barrier(values.astype(jnp.bfloat16)).astype(jnp.float32)


def conv_silu(values, taps):
    width = taps.shape[0] - 1
    length_all = values.shape[0]
    padded = jnp.pad(values, ((width - 1, 0), (0, 0)))
    mixed_sum = taps[width] + taps[0] * padded[0:length_all]
    for offset in range(1, width):
        mixed_sum = mixed_sum + taps[offset] * padded[offset : offset + length_all]
    return jax.nn.silu(mixed_sum)


def scan_product(inputs, b_matrix, c_matrix, step_sizes, decay):
    length_all, head_count, head_size = inputs.shape
    state_size = b_matrix.shape[1]
    block_count = length_all // SCAN_BLOCK
    pieces = (
        inputs.reshape(block_count, SCAN_BLOCK, head_count, head_size),
        b_matrix.reshape(block_count, SCAN_BLOCK, state_size),
        c_matrix.reshape(block_count, SCAN_BLOCK, state_size),
        step_sizes.reshape(block_count, SCAN_BLOCK, head_count),
    )
    causal = (jnp.arange(SCAN_BLOCK)[:, None] >= jnp.arange(SCAN_BLOCK)[None, :])[:, :, None]

    def advance(carried, block_in):
        x_part, b_part, c_part, step_part = block_in
        log_rates = -step_part * decay[None, :]
        running = jnp.cumsum(log_rates, axis=0)
        spread = running[:, None, :] - running[None, :, :]
        within = jnp.where(causal, jnp.exp(jnp.where(causal, spread, 0.0)), 0.0)
        scores = jnp.einsum("tn,sn->ts", c_part, b_part, precision=HIGH)
        mixing = scores[:, :, None] * within * step_part[None, :, :]
        local_out = jnp.einsum("tsh,shp->thp", mixing, x_part, precision=HIGH)
        from_state = jnp.exp(running)[:, :, None] * jnp.einsum(
            "tn,hnp->thp", c_part, carried, precision=HIGH
        )
        remain = jnp.exp(running[-1][None, :] - running) * step_part
        carried = jnp.exp(running[-1])[:, None, None] * carried + jnp.einsum(
            "sh,sn,shp->hnp", remain, b_part, x_part, precision=HIGH
        )
        return (carried, local_out + from_state)

    initial = jnp.zeros((head_count, state_size, head_size), jnp.float32)
    final_state, outputs = lax.scan(jax.checkpoint(advance), initial, pieces)
    return outputs.reshape(length_all, head_count, head_size)


def ssd_core(live_rows, x_in, bc_in, dt_in, bias_in, alog_in, skip_in):
    length_all = x_in.shape[0]
    heads_local = dt_in.shape[1]
    state_size = bc_in.shape[1] // 2
    step_sizes = jax.nn.softplus(dt_in + bias_in) * live_rows[:, None]
    x_heads = x_in.reshape(length_all, heads_local, x_in.shape[1] // heads_local)
    mixed_heads = (
        scan_product(
            x_heads, bc_in[:, :state_size], bc_in[:, state_size:], step_sizes, jnp.exp(alog_in)
        )
        + skip_in[None, :, None] * x_heads
    )
    return mixed_heads.reshape(length_all, x_in.shape[1])


def place_slice(values, start, full_len, axis_dim):
    shape_full = list(values.shape)
    shape_full[axis_dim] = full_len
    return lax.dynamic_update_slice_in_dim(
        jnp.zeros(shape_full, jnp.float32), values, start, axis_dim
    )


def local(
    hidden_in,
    lengths,
    order,
    in_gain,
    w_z,
    w_x,
    w_bc,
    w_dt,
    conv_x,
    conv_bc,
    dt_bias,
    a_log,
    d_skip,
    gated_gain,
    w_out,
    cotangent,
):
    dp_count = lax.axis_size("dp")
    tensor_count = lax.axis_size("tensor")
    dp_index = lax.axis_index("dp")
    tensor_index = lax.axis_index("tensor")
    piece_len = hidden_in.shape[2]
    model_width = hidden_in.shape[3]
    part_len = piece_len * tensor_count
    length_all = part_len * dp_count
    inner_local = w_z.shape[2]
    heads_local = w_dt.shape[2]
    state_size = w_bc.shape[2] // 2
    layer_count = w_z.shape[0]
    inner_all = inner_local * tensor_count
    heads_all = heads_local * tensor_count
    seq_length = jnp.take(lengths, jnp.take(order, dp_index))
    arranged = jnp.take(hidden_in, order, axis=0)
    dealt = lax.all_to_all(arranged, "dp", split_axis=0, concat_axis=1, tiled=True)
    hidden = dealt[0].astype(jnp.float32)
    positions = (
        jnp.arange(dp_count)[:, None] * part_len
        + tensor_index * piece_len
        + jnp.arange(piece_len)[None, :]
    )
    live_piece = (positions < seq_length).astype(jnp.float32)[:, :, None]
    live_rows = (jnp.arange(length_all) < seq_length).astype(jnp.float32)
    first_tensor = (tensor_index == 0).astype(jnp.float32)
    head_start = tensor_index * heads_local
    inner_start = tensor_index * inner_local
    gathered = (
        lax.all_gather(w_z, "dp", axis=1, tiled=True),
        lax.all_gather(w_x, "dp", axis=1, tiled=True),
        lax.all_gather(w_bc, "dp", axis=1, tiled=True),
        lax.all_gather(w_dt, "dp", axis=1, tiled=True),
        lax.all_gather(w_out, "dp", axis=1, tiled=True),
    )
    wide = (
        lax.all_gather(gathered[0][:, None], "tensor", axis=1, tiled=True),
        lax.all_gather(gathered[1][:, None], "tensor", axis=1, tiled=True),
        lax.all_gather(gathered[3][:, None], "tensor", axis=1, tiled=True),
        lax.all_gather(gathered[4][:, None], "tensor", axis=1, tiled=True),
    )
    saved = []
    for layer_idx in range(layer_count):
        g_z, g_x, g_bc, g_dt, g_out = (stacked[layer_idx] for stacked in gathered)
        w_heads = jnp.concatenate([g_z, g_x, g_dt], axis=1)
        inv_rms = lax.rsqrt(jnp.mean(hidden * hidden, axis=-1, keepdims=True) + EPS)
        normed_piece = (hidden * inv_rms * in_gain[layer_idx]).astype(jnp.bfloat16)
        normed = lax.all_gather(normed_piece, "tensor", axis=1, tiled=True).reshape(
            length_all, model_width
        )
        projected = jnp.dot(normed, w_heads, preferred_element_type=jnp.float32)
        gate_in = projected[:, :inner_local]
        x_raw = projected[:, inner_local : 2 * inner_local]
        dt_raw = projected[:, 2 * inner_local :]
        bc_raw = jnp.dot(normed, g_bc, preferred_element_type=jnp.float32)
        taps_x = lax.dynamic_slice_in_dim(conv_x[layer_idx], inner_start, inner_local, 1)
        x_conv, back_x = jax.vjp(conv_silu, x_raw, taps_x)
        bc_conv, back_bc = jax.vjp(conv_silu, bc_raw, conv_bc[layer_idx])
        bias_local = lax.dynamic_slice_in_dim(dt_bias[layer_idx], head_start, heads_local, 0)
        alog_local = lax.dynamic_slice_in_dim(a_log[layer_idx], head_start, heads_local, 0)
        skip_local = lax.dynamic_slice_in_dim(d_skip[layer_idx], head_start, heads_local, 0)
        mixed, back_core = jax.vjp(
            partial(ssd_core, live_rows),
            rounded(x_conv),
            rounded(bc_conv),
            dt_raw,
            bias_local,
            alog_local,
            skip_local,
        )
        gate_act = jax.nn.silu(gate_in)
        gated_mix = mixed * gate_act
        squares = lax.psum(jnp.sum(gated_mix * gated_mix, axis=-1), "tensor")
        gate_rms = lax.rsqrt(squares / inner_all + EPS)[:, None]
        gain_local = lax.dynamic_slice_in_dim(gated_gain[layer_idx], inner_start, inner_local, 0)
        gated_out = (gated_mix * gate_rms * gain_local).astype(jnp.bfloat16)
        received = lax.all_to_all(
            gated_out.reshape(dp_count, tensor_count, piece_len, inner_local),
            "tensor",
            split_axis=1,
            concat_axis=1,
            tiled=True,
        )
        branch = jnp.einsum(
            "aspc,sdc->apd", received, wide[3][layer_idx], preferred_element_type=jnp.float32
        )
        saved.append(
            (
                hidden,
                inv_rms,
                normed,
                gate_in,
                mixed,
                gate_act,
                gated_mix,
                gate_rms,
                gated_out,
                back_x,
                back_bc,
                back_core,
                gain_local,
            )
        )
        hidden = (hidden + branch) * live_piece
    block_out = hidden.astype(jnp.bfloat16)[None]
    grad_hidden = cotangent[0].astype(jnp.float32)
    layer_sums = [None] * layer_count
    small_lists = [[None] * layer_count for member in range(7)]
    for layer_idx in reversed(range(layer_count)):
        (
            hidden_prev,
            inv_rms,
            normed,
            gate_in,
            mixed,
            gate_act,
            gated_mix,
            gate_rms,
            gated_out,
            back_x,
            back_bc,
            back_core,
            gain_local,
        ) = saved[layer_idx]
        g_z, g_x, g_bc, g_dt, g_out = (stacked[layer_idx] for stacked in gathered)
        w_heads = jnp.concatenate([g_z, g_x, g_dt], axis=1)
        branch_grad = grad_hidden * live_piece
        grad_rows = lax.all_gather(
            branch_grad.astype(jnp.bfloat16), "tensor", axis=1, tiled=True
        ).reshape(length_all, model_width)
        grad_gated = jnp.dot(grad_rows, g_out, preferred_element_type=jnp.float32)
        grad_out_layer = lax.dot_general(
            grad_rows, gated_out, CONTRACT_FIRST, preferred_element_type=jnp.float32
        )
        grad_gain_layer = jnp.sum(grad_gated * gated_mix * gate_rms, axis=0)
        scaled_back = grad_gated * gain_local
        along = lax.psum(jnp.sum(scaled_back * gated_mix, axis=-1), "tensor")
        grad_mix = scaled_back * gate_rms - gated_mix * gate_rms**3 * (along[:, None] / inner_all)
        grad_mixed = grad_mix * gate_act
        sigmoid_gate = jax.nn.sigmoid(gate_in)
        grad_gate = grad_mix * mixed * sigmoid_gate * (1.0 + gate_in * (1.0 - sigmoid_gate))
        grad_x_low, grad_bc_part, grad_dt, grad_bias, grad_alog, grad_skip = back_core(grad_mixed)
        grad_bc = lax.psum(grad_bc_part.astype(jnp.bfloat16), "tensor").astype(jnp.float32)
        grad_x_raw, grad_taps_x = back_x(grad_x_low)
        grad_bc_raw, grad_taps_bc = back_bc(grad_bc)
        heads_grad = jnp.concatenate([grad_gate, grad_x_raw, grad_dt], axis=1).astype(jnp.bfloat16)
        bc_grad_low = grad_bc_raw.astype(jnp.bfloat16)
        received_grad = lax.all_to_all(
            heads_grad.reshape(dp_count, tensor_count, piece_len, heads_grad.shape[1]),
            "tensor",
            split_axis=1,
            concat_axis=1,
            tiled=True,
        )
        heads_full = jnp.concatenate(
            [wide[0][layer_idx], wide[1][layer_idx], wide[2][layer_idx]], axis=2
        )
        grad_normed = jnp.einsum(
            "aspc,sdc->apd", received_grad, heads_full, preferred_element_type=jnp.float32
        )
        bc_mine = lax.dynamic_slice_in_dim(
            bc_grad_low.reshape(dp_count, part_len, 2 * state_size),
            tensor_index * piece_len,
            piece_len,
            1,
        )
        grad_normed = grad_normed + lax.dot_general(
            bc_mine, g_bc, (((2,), (1,)), ((), ())), preferred_element_type=jnp.float32
        )
        grad_w_heads = lax.dot_general(
            normed, heads_grad, CONTRACT_FIRST, preferred_element_type=jnp.float32
        )
        grad_bc_layer = lax.dot_general(
            normed, bc_grad_low, CONTRACT_FIRST, preferred_element_type=jnp.float32
        )
        layer_terms = (
            grad_w_heads[:, :inner_local],
            grad_w_heads[:, inner_local : 2 * inner_local],
            grad_bc_layer,
            grad_w_heads[:, 2 * inner_local :],
            grad_out_layer,
        )
        layer_sums[layer_idx] = layer_terms
        grad_in_gain_layer = jnp.sum(grad_normed * hidden_prev * inv_rms, axis=(0, 1))
        scaled = grad_normed * in_gain[layer_idx]
        grad_hidden = (
            branch_grad
            + inv_rms * scaled
            - hidden_prev * inv_rms**3 * jnp.mean(scaled * hidden_prev, axis=-1, keepdims=True)
        )
        small_lists[0][layer_idx] = grad_in_gain_layer
        small_lists[1][layer_idx] = place_slice(grad_taps_x, inner_start, inner_all, 1)
        small_lists[2][layer_idx] = grad_taps_bc * first_tensor
        small_lists[3][layer_idx] = place_slice(grad_bias, head_start, heads_all, 0)
        small_lists[4][layer_idx] = place_slice(grad_alog, head_start, heads_all, 0)
        small_lists[5][layer_idx] = place_slice(grad_skip, head_start, heads_all, 0)
        small_lists[6][layer_idx] = place_slice(grad_gain_layer, inner_start, inner_all, 0)
    stacked_grads = tuple(
        (
            jnp.stack([layer_sums[layer_idx][member] for layer_idx in range(layer_count)])
            for member in range(5)
        )
    )
    summed_grads = lax.psum_scatter(stacked_grads, "dp", scatter_dimension=1, tiled=True)
    small_stacks = tuple((jnp.stack(small_lists[member]) for member in range(7)))
    small_sums = lax.psum(small_stacks, ("dp", "tensor"))
    returned = lax.all_to_all(
        grad_hidden.astype(jnp.bfloat16)[None], "dp", split_axis=1, concat_axis=0, tiled=True
    )
    input_grad = jnp.zeros_like(returned).at[order].set(returned)
    return (
        block_out,
        input_grad,
        small_sums[0],
        summed_grads[0],
        summed_grads[1],
        summed_grads[2],
        summed_grads[3],
        small_sums[1],
        small_sums[2],
        small_sums[3],
        small_sums[4],
        small_sums[5],
        small_sums[6],
        summed_grads[4],
    )


def solution(mesh):
    return jax.shard_map(
        local,
        mesh=mesh,
        in_specs=(
            P(None, "dp", "tensor", None),
            P(),
            P(),
            P(),
            P(None, "dp", "tensor"),
            P(None, "dp", "tensor"),
            P(None, "dp", None),
            P(None, "dp", "tensor"),
            P(),
            P(),
            P(),
            P(),
            P(),
            P(),
            P(None, "dp", "tensor"),
            P("dp", None, "tensor", None),
        ),
        out_specs=(
            P("dp", None, "tensor", None),
            P(None, "dp", "tensor", None),
            P(),
            P(None, "dp", "tensor"),
            P(None, "dp", "tensor"),
            P(None, "dp", None),
            P(None, "dp", "tensor"),
            P(),
            P(),
            P(),
            P(),
            P(),
            P(),
            P(None, "dp", "tensor"),
        ),
        check_vma=False,
    )
```

profile of v0, /device:TPU:0, one launch (start us, length us, event | category | flops | bytes accessed | tf_op | source)
XLA Modules:
  0.0 2002.7 jit_solution(15198110654869341422)
XLA Ops:
  19.8 24.8 %all-to-all-done = bf16[8,1,64,768]{3,2,1,0:T(8,128)(2,1)S(1)} async-done(((bf16[8,1,64,768]{3,2,1,0:T(8,128)(2,1)}), bf16[8,1,64,768]{3,2,1,0:T(8,128)(2,1)S(1)}, u32[]{:S(2)}, u32[]{:S(2)}) %all-to-all-start) | async-done | bytes 786464 | tf_op jit(solution)/shard_map/all_to_all | solution.py:122
  46.7 13.6 all-gather.21.cloned.1.call-done
  62.4 31.3 %all_gather.42 = bf16[2,768,6]{2,0,1:T(2,128)(2,1)S(1)} all-gather(bf16[2,96,6]{2,0,1:T(2,128)(2,1)S(1)} %copy.614), channel_id=1, replica_groups=mesh['dp'=8,'tensor'=4] {'dp'}, dimensions={1}, use_global_device_ids=true | all-gather | bytes 20736 | tf_op jit(solution)/shard_map/all_gather | solution.py:138
  101.1 32.2 %all_gather.43 = bf16[2,768,256]{2,1,0:T(8,128)(2,1)S(1)} all-gather(bf16[2,96,256]{2,1,0:T(8,128)(2,1)S(1)} %copy-done.69), channel_id=1, replica_groups=mesh['dp'=8,'tensor'=4] {'dp'}, dimensions={1}, use_global_device_ids=true | all-gather | bytes 884736 | tf_op jit(solution)/shard_map/all_gather | solution.py:137
  135.8 11.6 all-gather.19.cloned.1.call-done
  149.6 27.1 %all-gather.15.cloned.1.call-done = bf16[8,256,768]{2,1,0:T(8,128)(2,1)} async-done(((bf16[8,64,768]{2,1,0:T(8,128)(2,1)}), bf16[8,256,768]{2,1,0:T(8,128)(2,1)}) %all-gather.15.cloned.1.call-update) | async-done | bytes 3145744 | tf_op jit(solution)/shard_map/all_gather | solution.py:153
  198.3 151.5 %while.90 = (s32[]{:T(128)}, f32[6,128,64]{1,2,0:T(8,128)S(1)}, f32[8,256,6,64]{1,0,3,2:T(8,128)}, f32[8,6,128,64]{2,3,1,0:T(8,128)}, f32[8,256,6]{1,2,0:T(8,128...) while((s32[]{:T(128)}, f32[6,128,64]{1,2,0:T(8,128)S(1)}, ...), condition=%wide.region_4.6_spmd.clone.clone, body=%wide.region_1.0_spmd.clone.clone.sunk | while | flops 707254272 | bytes 5970259 | solution.py:61
  205.9 9.9 dynamic_update_slice.199
  224.8 9.9 dynamic_update_slice.199
  243.8 9.9 dynamic_update_slice.199
  385.0 15.0 all-to-all-done.1
  420.1 13.9 all-gather.23.cloned.1.call-done
  456.4 151.5 %while.91 = (s32[]{:T(128)}, f32[6,128,64]{1,2,0:T(8,128)S(1)}, f32[8,256,6,64]{1,0,3,2:T(8,128)}, f32[8,6,128,64]{2,3,1,0:T(8,128)}, f32[8,256,6]{1,2,0:T(8,128...) while((s32[]{:T(128)}, f32[6,128,64]{1,2,0:T(8,128)S(1)}, ...), condition=%wide.region_11.13_spmd.clone.clone, body=%wide.region_8.12_spmd.clone.clone.sunk | while | flops 707254272 | bytes 5970259 | solution.py:61
  463.9 9.9 dynamic_update_slice.201
  650.2 293.5 %while.88 = (s32[]{:T(128)}, f32[6]{0:T(128)S(1)}, f32[6,128,64]{1,2,0:T(8,128)S(1)}, f32[8,256,6,64]{1,0,3,2:T(8,128)}, f32[8,256,128]{2,1,0:T(8,128)}, /*index...) while((s32[]{:T(128)}, f32[6]{0:T(128)S(1)}, ...), condition=%wide.region_29.31_spmd.clone, body=%wide.region_16.30_spmd.clone.sunk | while | flops 1670431744 | bytes 15717104 | solution.py:61
  984.9 42.2 %all-reduce.57.cloned.1.call-done = bf16[2048,256]{1,0:T(8,128)(2,1)} async-done(((bf16[2048,256]{1,0:T(8,128)(2,1)}), bf16[2048,256]{1,0:T(8,128)(2,1)}) %all-reduce.57.cloned.1.call-update) | async-done | bytes 1048592 | tf_op jit(solution)/shard_map/psum | solution.py:248
  1059.3 12.5 all-gather.27.cloned.1.call-done
  1098.1 299.1 %while.89 = (s32[]{:T(128)}, f32[6]{0:T(128)S(1)}, f32[6,128,64]{1,2,0:T(8,128)S(1)}, f32[8,256,6,64]{1,0,3,2:T(8,128)}, f32[8,256,128]{2,1,0:T(8,128)}, /*index...) while((s32[]{:T(128)}, f32[6]{0:T(128)S(1)}, ...), condition=%wide.region_47.49_spmd.clone, body=%wide.region_34.48_spmd.clone.sunk | while | flops 1670431744 | bytes 15717104 | solution.py:61
  1447.6 31.2 %all-reduce.59.cloned.1.call-done = bf16[2048,256]{1,0:T(8,128)(2,1)} async-done(((bf16[2048,256]{1,0:T(8,128)(2,1)}), bf16[2048,256]{1,0:T(8,128)(2,1)}) %all-reduce.59.cloned.1.call-update) | async-done | bytes 1048592 | tf_op jit(solution)/shard_map/psum | solution.py:248
  1542.1 17.2 all-to-all-done.2
  1572.2 105.7 %all-reduce.61.cloned.1.call-done = (f32[2,768]{1,0:T(2,128)}, f32[2,5,1536]{2,0,1:T(2,128)}, f32[2,5,256]{2,1,0:T(8,128)}, f32[2,24]{1,0:T(2,128)}, f32[2,24]{1...) async-done(((f32[2,768]{1,0:T(2,128)}, f32[2,5,1536]{2,0,1:T(2,128)}, f32[2,5,256]{2,1,0:T(8,128)}, f32[2,24]{1,0:T(2,128)}, f32[2,24]{1,0:T(2,128)}, ...) | async-done | bytes 90704 | tf_op jit(solution)/shard_map/psum | solution.py:311
  1680.3 172.3 %all-reduce.63.cloned.1.call-done = (f32[2,768,384]{2,0,1:T(2,128)}, f32[2,768,384]{2,0,1:T(2,128)}) async-done(((f32[2,768,384]{2,0,1:T(2,128)}, f32[2,768,384]{2,0,1:T(2,128)}), (f32[2,768,384]{2,0,1:T(2,128)}, f32[2,768,384]{2,0,1:T(2,128)})) %all-reduce.63.cloned.1.call-update) | async-done | bytes 4718608
  1856.1 64.1 %reduce-scatter.6.cloned.1.call-done = f32[2,96,256]{2,1,0:T(8,128)} async-done(((f32[2,768,256]{2,1,0:T(8,128)}), f32[2,96,256]{2,1,0:T(8,128)}) %reduce-scatter.6.cloned.1.call-update) | async-done | bytes 196624 | tf_op jit(solution)/shard_map/reduce_scatter | solution.py:309
  1920.1 72.3 %reduce-scatter.8.cloned.1.call-done = f32[2,96,384]{2,1,0:T(8,128)} async-done(((f32[2,768,384]{2,1,0:T(8,128)}), f32[2,96,384]{2,1,0:T(8,128)}) %reduce-scatter.8.cloned.1.call-update) | async-done | bytes 294928 | tf_op jit(solution)/shard_map/reduce_scatter | solution.py:309
  (1636 shorter events, 1253.5 us)
Async XLA Ops:
  7.2 53.1 %all-gather.21.cloned.1.call-start = ((), (), s32[]{:S(2)}) async-start(), calls=%async_computation.12 | async-start | bytes 1327104 | tf_op jit(solution)/shard_map/all_gather | solution.py:139
  7.9 125.4 %all-gather.17.cloned.1.call-start = ((), (), s32[]{:S(2)}) async-start(), calls=%async_computation.10 | async-start | bytes 1327104 | tf_op jit(solution)/shard_map/all_gather | solution.py:135
  8.7 138.7 %all-gather.19.cloned.1.call-start = ((), (), s32[]{:S(2)}) async-start(), calls=%async_computation.11 | async-start | bytes 1327104 | tf_op jit(solution)/shard_map/all_gather | solution.py:136
  12.4 32.2 %all-to-all-start = ((bf16[8,1,64,768]{3,2,1,0:T(8,128)(2,1)}), bf16[8,1,64,768]{3,2,1,0:T(8,128)(2,1)S(1)}, u32[]{:S(2)}, u32[]{:S(2)}) async-start(bf16[8,1,64,768]{3,2,1,0:T(8,128)(2,1)} %bitcast_select_fusion), calls=%async_computation | async-start | bytes 1572864 | tf_op jit(solution)/shard_map/all_to_all | solution.py:122
  19.7 157.0 %all-gather.15.cloned.1.call-start = ((), (), s32[]{:S(2)}) async-start(), calls=%async_computation.9 | async-start | bytes 3932160 | tf_op jit(solution)/shard_map/all_gather | solution.py:153
  46.7 333.9 %all-gather.29.cloned.1.call-start = ((), (), s32[]{:S(2)}) async-start(), calls=%async_computation.20 | async-start | bytes 5898240 | tf_op jit(solution)/shard_map/all_gather | solution.py:145
  60.4 354.6 %all-gather.31.cloned.1.call-start = ((), (), s32[]{:S(2)}) async-start(), calls=%async_computation.21 | async-start | bytes 5898240 | tf_op jit(solution)/shard_map/all_gather | solution.py:142
  375.5 24.5 %all-to-all-start.1 = ((bf16[8,4,64,384]{3,2,0,1:T(8,128)(2,1)}), bf16[8,4,64,384]{3,2,0,1:T(8,128)(2,1)}, u32[]{:S(2)}, u32[]{:S(2)}) async-start(bf16[8,4,64,384]{3,2,0,1:T(8,128)(2,1)} %copy.621), calls=%async_computation.1 | async-start | bytes 3145728 | tf_op jit(solution)/shard_map/all_to_all | solution.py:182
  379.9 54.1 %all-gather.23.cloned.1.call-start = ((), (), s32[]{:S(2)}) async-start(), calls=%async_computation.13 | async-start | bytes 3932160 | tf_op jit(solution)/shard_map/all_gather | solution.py:153
  405.3 218.3 %all-gather.25.cloned.1.call-start = ((), (), s32[]{:S(2)}) async-start(), calls=%async_computation.14 | async-start | bytes 3932160 | tf_op jit(solution)/shard_map/all_gather | solution.py:233
  406.6 565.9 %all-gather.33.cloned.1.call-start = ((), (), s32[]{:S(2)}) async-start(), calls=%async_computation.22 | async-start | bytes 5898240 | tf_op jit(solution)/shard_map/all_gather | solution.py:143
  966.3 66.8 %all-to-all-start.3 = ((bf16[8,4,64,774]{3,2,0,1:T(8,128)(2,1)}), bf16[8,4,64,774]{3,2,0,1:T(8,128)(2,1)}, u32[]{:S(2)}, u32[]{:S(2)}) async-start(bf16[8,4,64,774]{3,2,0,1:T(8,128)(2,1)} %copy.637), calls=%async_computation.3 | async-start | bytes 7340032 | tf_op jit(solution)/shard_map/all_to_all | solution.py:253
  971.2 55.9 %all-reduce.57.cloned.1.call-start = ((), (), s32[]{:S(2)}) async-start(), calls=%async_computation.15 | async-start | bytes 2097152 | tf_op jit(solution)/shard_map/psum | solution.py:248
  972.4 99.4 %all-gather.27.cloned.1.call-start = ((), (), s32[]{:S(2)}) async-start(), calls=%async_computation.16 | async-start | bytes 3932160 | tf_op jit(solution)/shard_map/all_gather | solution.py:233
  1043.0 435.8 %all-reduce.59.cloned.1.call-start = ((), (), s32[]{:S(2)}) async-start(), calls=%async_computation.17 | async-start | bytes 2097152 | tf_op jit(solution)/shard_map/psum | solution.py:248
  1432.3 61.1 %all-to-all-start.4 = ((bf16[8,4,64,774]{3,2,0,1:T(8,128)(2,1)}), bf16[8,4,64,774]{3,2,0,1:T(8,128)(2,1)}, u32[]{:S(2)}, u32[]{:S(2)}) async-start(bf16[8,4,64,774]{3,2,0,1:T(8,128)(2,1)} %copy.650), calls=%async_computation.4 | async-start | bytes 7340032 | tf_op jit(solution)/shard_map/all_to_all | solution.py:253
  1437.2 133.4 %reduce-scatter.10.cloned.1.call-start = ((), (), s32[]{:S(2)}) async-start(), calls=%async_computation.23 | async-start | bytes 442368
  1440.6 237.3 %all-reduce.61.cloned.1.call-start = ((), (), s32[]{:S(2)}) async-start(), calls=%async_computation.24 | async-start | bytes 198656 | tf_op jit(solution)/shard_map/psum | solution.py:311
  1502.9 349.6 %all-reduce.63.cloned.1.call-start = ((), (), s32[]{:S(2)}) async-start(), calls=%async_computation.25 | async-start | bytes 9437184
  1515.3 404.9 %reduce-scatter.6.cloned.1.call-start = ((), (), s32[]{:S(2)}) async-start(), calls=%async_computation.18 | async-start | bytes 1769472 | tf_op jit(solution)/shard_map/reduce_scatter | solution.py:309
  1521.9 470.6 %reduce-scatter.8.cloned.1.call-start = ((), (), s32[]{:S(2)}) async-start(), calls=%async_computation.19 | async-start | bytes 2654208 | tf_op jit(solution)/shard_map/reduce_scatter | solution.py:309
  1534.4 25.0 %all-to-all-start.2 = ((bf16[8,4,64,384]{3,2,0,1:T(8,128)(2,1)}), bf16[8,4,64,384]{3,2,0,1:T(8,128)(2,1)}, u32[]{:S(2)}, u32[]{:S(2)}) async-start(bf16[8,4,64,384]{3,2,0,1:T(8,128)(2,1)} %copy.628), calls=%async_computation.2 | async-start | bytes 3145728 | tf_op jit(solution)/shard_map/all_to_all | solution.py:182
  1559.3 119.8 %all-to-all-start.5 = ((bf16[1,8,64,768]{3,2,0,1:T(8,128)(2,1)}), bf16[1,8,64,768]{3,2,0,1:T(8,128)(2,1)S(1)}, u32[]{:S(2)}, u32[]{:S(2)}) async-start(bf16[1,8,64,768]{3,2,0,1:T(8,128)(2,1)} %fusion.271), calls=%async_computation.5 | async-start | bytes 1572864 | tf_op jit(solution)/shard_map/all_to_all | solution.py:312
  1679.2 316.8 %copy-start.1 = (bf16[8,1,64,768]{3,2,1,0:T(8,128)(2,1)S(1)}, bf16[8,1,64,768]{3,2,1,0:T(8,128)(2,1)}, u32[]{:S(2)}) copy-start(bf16[8,1,64,768]{3,2,1,0:T(8,128)(2,1)} %param.25) | copy-start | bytes 2359300
  (141 other events, 4424.9 us)
Sparse Core Ops, SparseCore 0:
  10.2 50.0 all-gather.20
  62.5 41.5 all-gather.16
  106.4 41.0 all-gather.18
  149.4 27.2 all-gather.14
  178.2 37.4 all-gather.28
  217.1 37.4 all-gather.30
  405.5 28.4 all-gather.22
  435.6 28.5 all-gather.24
  465.7 37.4 all-gather.32
  974.1 52.9 all-reduce.56
  1043.2 28.5 all-gather.26
  1428.6 50.1 all-reduce.58
  1482.1 61.4 reduce-scatter.9
  1551.0 126.8 all-reduce.60
  1681.3 171.1 all-reduce.62
  1856.4 63.7 reduce-scatter.5
  1924.5 67.9 reduce-scatter.7
where the time goes:
time: 2020 us; the launch traced here: 2000 us
  waiting for transfers between devices  633 us (31%)
  local copies, waits for them, and re-layouts  588 us (29%)
  other arithmetic  320 us (16%)
  matrix products  314 us (16%)
  blocking collectives  93.5 us (5%)
  starting transfers between devices  32.3 us (2%)
    dynamic_update_slice x64, local copies, waits for them, and re-layouts, scan_product(): final_state, outputs = lax.scan(jax.checkpoint(advance), initial, pieces)  328 us
    another operation x148, other arithmetic  192 us
    unnamed x19, waiting for transfers between devices  175 us
    reduce_scatter x2, waiting for transfers between devices, local(): lax.psum_scatter(stacked_grads, 'dp', scatter_dimension=1, tiled=True)  136 us
    dot_general x48, matrix products, advance(): local_out = jnp.einsum('tsh,shp->thp', mixing, x_part, precision=HIGH)  112 us
    psum x1, waiting for transfers between devices, local(): small_sums = lax.psum(small_stacks, ('dp', 'tensor'))  106 us
    psum x2, waiting for transfers between devices, local(): lax.psum(grad_bc_part.astype(jnp.bfloat16), 'tensor').astype(jnp.float32)  73.4 us
    squeeze x64, local copies, waits for them, and re-layouts, scan_product(): final_state, outputs = lax.scan(jax.checkpoint(advance), initial, pieces)  54 us
  transfers between devices with their start and end apart: 23, of which 15 were waited for; matrix products, arithmetic and copies ran while one was open for 43% of the time, Pallas kernels for 0%

commit v1 on v0

v1 whole, which is shorter than its diff:
```python
from functools import partial

import jax
import jax.numpy as jnp
from jax import lax
from jax.experimental import pallas as pl
from jax.experimental.pallas import tpu as pltpu
from jax.sharding import PartitionSpec as P

SCAN_BLOCK = 256
EPS = 1e-05
LOG2E = 1.4426950408889634
F32, BF16 = jnp.float32, jnp.bfloat16
LANES = 128
GROUP = 256
PAD = 16
ROWS = 128
WIDTH = 4
NN = (((1,), (0,)), ((), ()))
NT = (((1,), (1,)), ((), ()))


def mm(left, right, dims=NN):
    return lax.dot_general(left, right, dims, preferred_element_type=F32)


def exact(left, right):
    return lax.dot_general(
        left, right, NN, precision=lax.Precision.HIGHEST, preferred_element_type=F32
    )


def halves(values):
    high = values.astype(BF16)
    return high, (values - high.astype(F32)).astype(BF16)


def beside(values):
    return jnp.concatenate(halves(values), axis=1)


def lanes_of(step, size):
    return pl.ds(pl.multiple_of(step * size, size), size)


def conv_rows(raw, taps, start, columns):
    total = taps[WIDTH : WIDTH + 1, columns]
    for tap in range(WIDTH):
        first = PAD - (WIDTH - 1) + tap + start
        total = total + taps[tap : tap + 1, columns] * raw[pl.ds(first, ROWS), columns]
    return total


def step_terms(dtp, live, aneg, dt, run, run_t, step_two, grow_two, keep_two, decay, spread, block):
    rows = pl.ds(block * SCAN_BLOCK, SCAN_BLOCK)
    value = dtp[rows, :]
    size = (jnp.maximum(value, 0.0) + jnp.log1p(jnp.exp(-jnp.abs(value)))) * live[rows, :]
    dt[block] = size
    row_id = lax.broadcasted_iota(jnp.int32, (SCAN_BLOCK, SCAN_BLOCK), 0)
    col_id = lax.broadcasted_iota(jnp.int32, (SCAN_BLOCK, SCAN_BLOCK), 1)
    earlier = (row_id >= col_id).astype(F32)
    running = exact(earlier, size * (aneg[0:1, :] * LOG2E))
    run[block] = running
    run_t[block] = running.T
    total = running[SCAN_BLOCK - 1 : SCAN_BLOCK, :]
    step_two[block] = beside(size)
    grow_two[block] = beside(jnp.exp2(running))
    keep_two[block] = beside(jnp.exp2(total - running))
    whole = jnp.broadcast_to(jnp.exp2(total), (8, LANES))
    decay[block] = mm(beside(whole), spread[...])


def split_narrow(narrow, select, wbc, wdt):
    wbc[...] = mm(narrow[...], select[:, : wbc.shape[1]]).astype(BF16)
    wdt[...] = mm(narrow[...], select[:, wbc.shape[1] :]).astype(BF16)


def small_rows(width, inner, state):
    sizes = (
        ("heads", 8),
        ("gain", -(-width // LANES // 8) * 8),
        ("gate_gain", inner // LANES),
        ("tap_x", (WIDTH + 1) * (inner // LANES)),
        ("tap_b", (WIDTH + 1) * (2 * state // LANES)),
    )
    starts, total = {}, 0
    for name, size in sizes:
        starts[name] = total
        total += size
    starts["all"] = -(-total // 8) * 8
    return starts


def forward_kernel(
    n_tensor,
    n_blocks,
    head_size,
    h,
    gain,
    tap_x,
    tap_b,
    dt_bias,
    aneg,
    skip,
    gate_gain,
    live,
    spread,
    select,
    wz_in,
    wx_in,
    wn_in,
    wo_in,
    h_next,
    nx,
    gate,
    xraw,
    braw,
    xc,
    bc,
    dtp,
    mixed,
    states,
    rms,
    wz,
    wx,
    wn,
    wo,
    wbc,
    wdt,
    halo,
    dt,
    run,
    run_t,
    step_two,
    grow_two,
    keep_two,
    decay,
    pair,
    fresh,
    carry_out,
    carry_in,
    gm,
    go,
    squares,
    w_sem,
    halo_send,
    halo_recv,
    carry_send,
    carry_recv,
):
    me = lax.axis_index("tensor")
    tokens, width = h.shape
    inner = gate.shape[1]
    state = fresh.shape[1]
    groups = inner // GROUP
    per_group = GROUP // head_size

    loads = {
        "wz": pltpu.make_async_copy(wz_in, wz, w_sem.at[0]),
        "wx": pltpu.make_async_copy(wx_in, wx, w_sem.at[1]),
        "wo": pltpu.make_async_copy(wo_in, wo, w_sem.at[2]),
        "wn": pltpu.make_async_copy(wn_in, wn, w_sem.at[3]),
    }
    for load in loads.values():
        load.start()

    barrier = pltpu.get_barrier_semaphore()

    @pl.when(me > 0)
    def _():
        pl.semaphore_signal(
            barrier, inc=1, device_id={"tensor": me - 1}, device_id_type=pl.DeviceIdType.MESH
        )

    @pl.when(me < n_tensor - 1)
    def _():
        pl.semaphore_wait(barrier, 1)

    following = lax.rem(me + 1, n_tensor)
    halo_copy = pltpu.make_async_remote_copy(
        src_ref=h.at[pl.ds(tokens - PAD, PAD), :],
        dst_ref=halo,
        send_sem=halo_send,
        recv_sem=halo_recv,
        device_id={"tensor": following},
        device_id_type=pl.DeviceIdType.MESH,
    )
    carry_copies = [
        pltpu.make_async_remote_copy(
            src_ref=carry_out.at[group],
            dst_ref=carry_in.at[group],
            send_sem=carry_send.at[group],
            recv_sem=carry_recv.at[group],
            device_id={"tensor": following},
            device_id_type=pl.DeviceIdType.MESH,
        )
        for group in range(groups)
    ]

    @pl.when(me < n_tensor - 1)
    def _():
        halo_copy.start()

    def normalize(values):
        inv = lax.rsqrt(jnp.mean(values * values, axis=-1, keepdims=True) + EPS)
        return (values * inv * gain[0:1, :]).astype(BF16)

    @pl.loop(0, tokens // ROWS)
    def _(step):
        rows = pl.ds(pl.multiple_of(step * ROWS, ROWS), ROWS)
        nx[pl.ds(pl.multiple_of(PAD + step * ROWS, PAD), ROWS), :] = normalize(h[rows, :])

    loads["wz"].wait()

    @pl.loop(0, groups)
    def _(step):
        columns = lanes_of(step, GROUP)
        gate[:, columns] = mm(nx[pl.ds(PAD, tokens), :], wz[:, columns])

    @pl.when(me > 0)
    def _():
        halo_copy.wait_recv()
        nx[0:PAD, :] = normalize(halo[...])

    @pl.when(me == 0)
    def _():
        nx[0:PAD, :] = jnp.zeros((PAD, width), BF16)

    loads["wx"].wait()

    def convolve(weights, taps, raw, out, columns):
        raw[:, columns] = mm(nx[...], weights[:, columns])
        for start in range(0, tokens, ROWS):
            before = conv_rows(raw, taps, start, columns)
            out[pl.ds(start, ROWS), columns] = (before * jax.nn.sigmoid(before)).astype(BF16)

    @pl.loop(0, groups)
    def _(step):
        convolve(wx, tap_x, xraw, xc, lanes_of(step, GROUP))

    loads["wn"].wait()
    split_narrow(wn, select, wbc, wdt)
    for step in range(bc.shape[1] // GROUP):
        convolve(wbc, tap_b, braw, bc, pl.ds(step * GROUP, GROUP))
    dtp[...] = mm(nx[pl.ds(PAD, tokens), :], wdt[...]) + dt_bias[0:1, :]

    row_id = lax.broadcasted_iota(jnp.int32, (SCAN_BLOCK, SCAN_BLOCK), 0)
    col_id = lax.broadcasted_iota(jnp.int32, (SCAN_BLOCK, SCAN_BLOCK), 1)
    head_of = lax.broadcasted_iota(jnp.int32, (SCAN_BLOCK, GROUP), 1) // head_size
    for block in range(n_blocks):
        step_terms(
            dtp, live, aneg, dt, run, run_t, step_two, grow_two, keep_two, decay, spread, block
        )
        rows = pl.ds(block * SCAN_BLOCK, SCAN_BLOCK)
        scores = mm(bc[rows, state:], bc[rows, :state], NT)
        pair[block] = jnp.where(row_id >= col_id, scores, 0.0)
        b_rows = bc[rows, :state].astype(F32).T.astype(BF16)

        @pl.loop(0, groups)
        def _(group):
            columns = lanes_of(group, GROUP)
            sizes = mm(step_two[block], spread[:, columns])
            keeps = mm(keep_two[block], spread[:, columns])
            weighted = (xc[rows, columns].astype(F32) * sizes * keeps).astype(BF16)
            fresh[block, :, columns] = mm(b_rows, weighted)

    for group in range(groups):
        columns = pl.ds(group * GROUP, GROUP)

        @pl.when(me > 0)
        def _():
            carry_copies[group].wait_recv()
            states[0, :, columns] = carry_in[group].astype(F32)

        @pl.when(me == 0)
        def _():
            states[0, :, columns] = jnp.zeros((state, GROUP), F32)

        for block in range(n_blocks):
            states[block + 1, :, columns] = (
                states[block, :, columns] * decay[block, 0:1, columns] + fresh[block, :, columns]
            )
        carry_out[group] = states[n_blocks, :, columns].astype(BF16)

        @pl.when(me < n_tensor - 1)
        def _():
            carry_copies[group].start()

    squares[...] = jnp.zeros_like(squares)
    for block in range(n_blocks):
        rows = pl.ds(block * SCAN_BLOCK, SCAN_BLOCK)

        @pl.loop(0, groups)
        def _(group):
            columns = lanes_of(group, GROUP)
            sizes = mm(step_two[block], spread[:, columns])
            grown = mm(grow_two[block], spread[:, columns])
            x_here = xc[rows, columns].astype(F32)
            stepped = (x_here * sizes).astype(BF16)
            rolled = pltpu.roll(run[block], lax.rem(LANES - per_group * group, LANES), 1)
            total = grown * mm(bc[rows, state:], states[block, :, columns].astype(BF16))
            total = total + skip[0:1, columns] * x_here
            for head in range(per_group):
                spread_out = (
                    rolled[:, head : head + 1] - run_t[block, pl.ds(per_group * group + head, 1), :]
                )
                mixing = (pair[block] * jnp.exp2(jnp.minimum(spread_out, 0.0))).astype(BF16)
                total = total + mm(mixing, jnp.where(head_of == head, stepped, jnp.zeros_like(stepped)))
            mixed[rows, columns] = total
            gate_in = gate[rows, columns]
            gated = total * gate_in * jax.nn.sigmoid(gate_in)
            gm[rows, columns] = gated
            squared = gated * gated
            for lane in range(0, GROUP, LANES):
                squares[rows, :] += squared[:, lane : lane + LANES]

    rms[...] = jnp.broadcast_to(
        lax.rsqrt(jnp.sum(squares[...], axis=-1, keepdims=True) / inner + EPS), rms.shape
    )

    @pl.loop(0, groups)
    def _(group):
        columns = lanes_of(group, GROUP)
        for start in range(0, tokens, ROWS):
            rows = pl.ds(start, ROWS)
            go[rows, columns] = (
                gm[rows, columns] * rms[rows, 0:1] * gate_gain[0:1, columns]
            ).astype(BF16)

    loads["wo"].wait()

    @pl.loop(0, width // GROUP)
    def _(step):
        columns = lanes_of(step, GROUP)
        branch = mm(go[...], wo[columns, :], NT)
        h_next[:, columns] = (h[:, columns] + branch) * live[:, 0:1]

    @pl.when(me < n_tensor - 1)
    def _():
        halo_copy.wait_send()
        for copy in carry_copies:
            copy.wait_send()


def backward_kernel(
    n_tensor,
    n_blocks,
    head_size,
    gh,
    h,
    gain,
    tap_x,
    tap_b,
    aneg,
    skip,
    gate_gain,
    live,
    spread,
    select,
    collect,
    nx,
    gate,
    xraw,
    braw,
    xc,
    bc,
    dtp,
    mixed,
    states,
    rms,
    wz_in,
    wx_in,
    wn_in,
    wo_in,
    gh_next,
    g_wz,
    g_wx,
    g_wo,
    g_narrow,
    g_small,
    wz,
    wx,
    wn,
    wo,
    wbc,
    wdt,
    g_branch,
    g_branch_t,
    normed_t,
    dt,
    run,
    run_t,
    step_two,
    grow_two,
    keep_two,
    decay,
    pair_t,
    g_pair_t,
    gq,
    gb,
    pz,
    px,
    pb,
    pd,
    fresh,
    d_states,
    carry_out,
    carry_in,
    g_heads,
    along,
    direct,
    g_run,
    d_b,
    d_c,
    gn,
    g_gain,
    w_sem,
    halo_send,
    halo_recv,
    carry_send,
    carry_recv,
):
    me = lax.axis_index("tensor")
    tokens, width = h.shape
    inner = gate.shape[1]
    state = fresh.shape[1]
    groups = inner // GROUP
    per_group = GROUP // head_size

    loads = {
        "wo": pltpu.make_async_copy(wo_in, wo, w_sem.at[0]),
        "wz": pltpu.make_async_copy(wz_in, wz, w_sem.at[1]),
        "wx": pltpu.make_async_copy(wx_in, wx, w_sem.at[2]),
        "wn": pltpu.make_async_copy(wn_in, wn, w_sem.at[3]),
    }
    for load in loads.values():
        load.start()

    barrier = pltpu.get_barrier_semaphore()

    @pl.when(me < n_tensor - 1)
    def _():
        pl.semaphore_signal(
            barrier, inc=1, device_id={"tensor": me + 1}, device_id_type=pl.DeviceIdType.MESH
        )

    @pl.when(me > 0)
    def _():
        pl.semaphore_wait(barrier, 1)

    previous = lax.rem(me + n_tensor - 1, n_tensor)
    carry_copies = [
        pltpu.make_async_remote_copy(
            src_ref=carry_out.at[group],
            dst_ref=carry_in.at[group],
            send_sem=carry_send.at[group],
            recv_sem=carry_recv.at[group],
            device_id={"tensor": previous},
            device_id_type=pl.DeviceIdType.MESH,
        )
        for group in range(groups)
    ]
    halo_copies = [
        pltpu.make_async_remote_copy(
            src_ref=buffer.at[pl.ds(0, PAD), :],
            dst_ref=buffer.at[pl.ds(tokens, PAD), :],
            send_sem=halo_send.at[index],
            recv_sem=halo_recv.at[index],
            device_id={"tensor": previous},
            device_id_type=pl.DeviceIdType.MESH,
        )
        for index, buffer in enumerate((gq, gb))
    ]

    @pl.loop(0, tokens // ROWS)
    def _(step):
        rows = pl.ds(pl.multiple_of(step * ROWS, ROWS), ROWS)
        low = (gh[rows, :] * live[rows, 0:1]).astype(BF16)
        g_branch[rows, :] = low
        columns = lanes_of(step, ROWS)
        g_branch_t[:, columns] = low.T
        normed_t[:, columns] = nx[pl.ds(pl.multiple_of(PAD + step * ROWS, PAD), ROWS), :].T

    for block in range(n_blocks):
        step_terms(
            dtp, live, aneg, dt, run, run_t, step_two, grow_two, keep_two, decay, spread, block
        )

    at = small_rows(width, inner, state)

    def put_small(name, row, tile, values):
        for lane in range(0, values.shape[1], LANES):
            g_small[pl.ds(at[name] + row + tile + lane // LANES, 1), :] = values[:, lane : lane + LANES]

    loads["wo"].wait()
    along[...] = jnp.zeros_like(along)

    @pl.loop(0, groups)
    def _(group):
        columns = lanes_of(group, GROUP)
        gained = jnp.zeros((1, GROUP), F32)
        gq[pl.ds(0, tokens), columns] = mm(g_branch[...], wo[:, columns])
        for start in range(0, tokens, ROWS):
            rows = pl.ds(start, ROWS)
            gate_in = gate[rows, columns]
            gated = mixed[rows, columns] * gate_in * jax.nn.sigmoid(gate_in)
            scaled = gated * rms[rows, 0:1]
            px[rows, columns] = (scaled * gate_gain[0:1, columns]).astype(BF16)
            g_gated = gq[rows, columns]
            gained = gained + jnp.sum(g_gated * scaled, axis=0, keepdims=True)
            back = g_gated * gate_gain[0:1, columns]
            gq[rows, columns] = back
            product = back * gated
            for lane in range(0, GROUP, LANES):
                along[rows, :] += product[:, lane : lane + LANES]
        put_small("gate_gain", 0, group * (GROUP // LANES), gained)
        g_wo[:, columns] = mm(g_branch_t[...], px[:, columns]).astype(BF16)

    along[...] = jnp.broadcast_to(
        jnp.sum(along[...], axis=-1, keepdims=True) / inner, along.shape
    )
    loads["wz"].wait()

    @pl.loop(0, groups)
    def _(group):
        columns = lanes_of(group, GROUP)
        for start in range(0, tokens, ROWS):
            rows = pl.ds(start, ROWS)
            gate_in = gate[rows, columns]
            sig = jax.nn.sigmoid(gate_in)
            act = gate_in * sig
            here = mixed[rows, columns]
            scale = rms[rows, 0:1]
            g_mix = scale * gq[rows, columns] - here * act * (scale * scale * scale * along[rows, 0:1])
            gq[rows, columns] = g_mix * act
            pz[rows, columns] = (g_mix * here * sig * (1.0 + gate_in * (1.0 - sig))).astype(BF16)
        g_wz[:, columns] = mm(normed_t[...], pz[:, columns]).astype(BF16)

    row_id = lax.broadcasted_iota(jnp.int32, (SCAN_BLOCK, SCAN_BLOCK), 0)
    col_id = lax.broadcasted_iota(jnp.int32, (SCAN_BLOCK, SCAN_BLOCK), 1)
    head_of = lax.broadcasted_iota(jnp.int32, (SCAN_BLOCK, GROUP), 1) // head_size
    for block in range(n_blocks):
        rows = pl.ds(block * SCAN_BLOCK, SCAN_BLOCK)
        scores = mm(bc[rows, :state], bc[rows, state:], NT)
        pair_t[block] = jnp.where(row_id <= col_id, scores, 0.0)
        c_rows = bc[rows, state:].astype(F32).T.astype(BF16)

        @pl.loop(0, groups)
        def _(group):
            columns = lanes_of(group, GROUP)
            grown = mm(grow_two[block], spread[:, columns])
            fresh[block, :, columns] = mm(c_rows, (gq[rows, columns] * grown).astype(BF16))

    for group in range(groups):
        columns = pl.ds(group * GROUP, GROUP)

        @pl.when(me < n_tensor - 1)
        def _():
            carry_copies[group].wait_recv()
            d_states[n_blocks, :, columns] = carry_in[group].astype(F32)

        @pl.when(me == n_tensor - 1)
        def _():
            d_states[n_blocks, :, columns] = jnp.zeros((state, GROUP), F32)

        for block in reversed(range(n_blocks)):
            d_states[block, :, columns] = (
                d_states[block + 1, :, columns] * decay[block, 0:1, columns]
                + fresh[block, :, columns]
            )
        carry_out[group] = d_states[0, :, columns].astype(BF16)

        @pl.when(me > 0)
        def _():
            carry_copies[group].start()

    g_heads[...] = jnp.zeros_like(g_heads)
    for block in range(n_blocks):
        rows = pl.ds(block * SCAN_BLOCK, SCAN_BLOCK)
        g_pair_t[...] = jnp.zeros_like(g_pair_t)
        d_b[...] = jnp.zeros_like(d_b)
        d_c[...] = jnp.zeros_like(d_c)
        direct[...] = jnp.zeros_like(direct)
        g_run[...] = jnp.zeros_like(g_run)

        @pl.loop(0, groups)
        def _(group):
            columns = lanes_of(group, GROUP)
            sizes = mm(step_two[block], spread[:, columns])
            grown = mm(grow_two[block], spread[:, columns])
            keeps = mm(keep_two[block], spread[:, columns])
            x_here = xc[rows, columns].astype(F32)
            stepped = (x_here * sizes).astype(BF16)
            g_out = gq[rows, columns]
            g_low = g_out.astype(BF16)
            rolled = pltpu.roll(run[block], lax.rem(LANES - per_group * group, LANES), 1)
            d_here = d_states[block + 1, :, columns].astype(BF16)
            d_x = keeps * mm(bc[rows, :state], d_here)
            d_b[...] += mm((x_here * sizes * keeps).astype(BF16), d_here, NT)
            d_c[...] += mm(
                (g_out * grown).astype(BF16), states[block, :, columns].astype(BF16), NT
            )
            for head in range(per_group):
                spread_out = (
                    run_t[block, pl.ds(per_group * group + head, 1), :] - rolled[:, head : head + 1]
                )
                factor = jnp.exp2(jnp.minimum(spread_out, 0.0))
                mixing = (pair_t[block] * factor).astype(BF16)
                g_one = jnp.where(head_of == head, g_low, jnp.zeros_like(g_low))
                d_x = d_x + mm(mixing, g_one)
                g_pair_t[...] += mm(stepped, g_one, NT) * factor
            skipped = skip[0:1, columns]
            toward = g_out * (mixed[rows, columns] - skipped * x_here) - stepped.astype(F32) * d_x
            for values, target in ((d_x * x_here, direct), (toward, g_run)):
                high, low = halves(values)
                target[...] += mm(high, collect[columns, :]) + mm(low, collect[columns, :])
            skip_sum = jnp.broadcast_to(
                jnp.sum(g_out * x_here, axis=0, keepdims=True), (8, GROUP)
            )
            high, low = halves(skip_sum)
            g_heads[2:3, :] += (mm(high, collect[columns, :]) + mm(low, collect[columns, :]))[0:1, :]
            gq[rows, columns] = sizes * d_x + skipped * g_out

        g_scores = jnp.where(row_id <= col_id, g_pair_t[...], 0.0)
        g_low = g_scores.astype(BF16)
        gb[rows, :state] = d_b[...] + mm(g_low, bc[rows, state:])
        gb[rows, state:] = d_c[...] + mm(g_scores.T.astype(BF16), bc[rows, :state])
        end_sum = jnp.broadcast_to(
            jnp.sum(d_states[block + 1] * states[block + 1], axis=0, keepdims=True), (8, inner)
        )
        high, low = halves(end_sum)
        at_end = (mm(high, collect[...]) + mm(low, collect[...]))[0:1, :]
        later = (row_id <= col_id).astype(F32)
        g_rate = exact(later, g_run[...]) + at_end
        value = dtp[rows, :]
        g_dt = (aneg[0:1, :] * g_rate + direct[...]) * live[rows, :] * jax.nn.sigmoid(value)
        pd[rows, :] = g_dt.astype(BF16)
        g_heads[0:1, :] += jnp.sum(g_dt, axis=0, keepdims=True)
        g_heads[1:2, :] += jnp.sum(g_rate * dt[block], axis=0, keepdims=True) * aneg[0:1, :]

    def before_conv(taps, raw, grad, columns):
        for start in range(0, tokens, ROWS):
            rows = pl.ds(start, ROWS)
            before = conv_rows(raw, taps, start, columns)
            sig = jax.nn.sigmoid(before)
            grad[rows, columns] = grad[rows, columns] * (sig * (1.0 + before * (1.0 - sig)))

    def through_conv(taps, raw, grad, columns, name, tile, low):
        sums = [jnp.zeros((1, GROUP), F32) for tap in range(WIDTH + 1)]
        for start in range(0, tokens, ROWS):
            total = jnp.zeros((ROWS, GROUP), F32)
            here = grad[pl.ds(start, ROWS), columns]
            for tap in range(WIDTH):
                shift = WIDTH - 1 - tap
                total = total + taps[tap : tap + 1, columns] * grad[pl.ds(start + shift, ROWS), columns]
                sums[tap] = sums[tap] + jnp.sum(
                    here * raw[pl.ds(PAD - shift + start, ROWS), columns], axis=0, keepdims=True
                )
            sums[WIDTH] = sums[WIDTH] + jnp.sum(here, axis=0, keepdims=True)
            low[pl.ds(start, ROWS), columns] = total.astype(BF16)
        for tap in range(WIDTH + 1):
            put_small(name, tap * (grad.shape[1] // LANES), tile, sums[tap])

    for step in range(bc.shape[1] // GROUP):
        before_conv(tap_b, braw, gb, pl.ds(step * GROUP, GROUP))

    @pl.loop(0, groups)
    def _(step):
        before_conv(tap_x, xraw, gq, lanes_of(step, GROUP))

    @pl.when(me > 0)
    def _():
        for copy in halo_copies:
            copy.start()

    g_narrow[:, 2 * state : 2 * state + LANES] = mm(normed_t[...], pd[...]).astype(BF16)
    g_narrow[:, 2 * state + LANES :] = jnp.zeros((width, LANES), BF16)
    loads["wx"].wait()
    loads["wn"].wait()
    split_narrow(wn, select, wbc, wdt)

    @pl.when(me < n_tensor - 1)
    def _():
        for copy in halo_copies:
            copy.wait_recv()

    @pl.when(me == n_tensor - 1)
    def _():
        for buffer in (gq, gb):
            buffer[pl.ds(tokens, PAD), :] = jnp.zeros((PAD, buffer.shape[1]), F32)

    for step in range(bc.shape[1] // GROUP):
        columns = pl.ds(step * GROUP, GROUP)
        through_conv(tap_b, braw, gb, columns, "tap_b", step * (GROUP // LANES), pb)
        g_narrow[:, columns] = mm(normed_t[...], pb[:, columns]).astype(BF16)

    @pl.loop(0, groups)
    def _(step):
        columns = lanes_of(step, GROUP)
        through_conv(tap_x, xraw, gq, columns, "tap_x", step * (GROUP // LANES), px)
        g_wx[:, columns] = mm(normed_t[...], px[:, columns]).astype(BF16)

    @pl.loop(0, width // GROUP)
    def _(step):
        columns = lanes_of(step, GROUP)
        gn[:, columns] = (
            mm(pz[...], wz[columns, :], NT)
            + mm(px[...], wx[columns, :], NT)
            + mm(pb[...], wbc[columns, :], NT)
            + mm(pd[...], wdt[columns, :], NT)
        )

    g_gain[...] = jnp.zeros_like(g_gain)
    g_small[pl.ds(at["heads"], 8), :] = g_heads[...]
    g_small[pl.ds(at["gain"], 8), :] = jnp.zeros((8, LANES), F32)

    @pl.loop(0, tokens // ROWS)
    def _(step):
        rows = pl.ds(pl.multiple_of(step * ROWS, ROWS), ROWS)
        values = h[rows, :]
        inv = lax.rsqrt(jnp.mean(values * values, axis=-1, keepdims=True) + EPS)
        g_normed = gn[rows, :]
        g_gain[0:1, :] += jnp.sum(g_normed * values * inv, axis=0, keepdims=True)
        scaled = g_normed * gain[0:1, :]
        along_h = jnp.mean(scaled * values, axis=-1, keepdims=True)
        gh_next[rows, :] = (
            gh[rows, :] * live[rows, 0:1] + inv * scaled - values * (inv * inv * inv * along_h)
        )

    put_small("gain", 0, 0, g_gain[0:1, :])

    @pl.when(me > 0)
    def _():
        for copy in halo_copies:
            copy.wait_send()
        for copy in carry_copies:
            copy.wait_send()


VMEM = pl.BlockSpec(memory_space=pltpu.VMEM)
ANY = pl.BlockSpec(memory_space=pl.ANY)


def shaped(shape, dtype=F32):
    return jax.ShapeDtypeStruct(shape, dtype)


def weight_scratch(width, inner, state, narrow):
    return [
        pltpu.VMEM((width, inner), BF16),
        pltpu.VMEM((width, inner), BF16),
        pltpu.VMEM((width, narrow), BF16),
        pltpu.VMEM((width, inner), BF16),
        pltpu.VMEM((width, 2 * state), BF16),
        pltpu.VMEM((width, LANES), BF16),
    ]


def block_scratch(n_blocks, inner):
    return [
        pltpu.VMEM((n_blocks, SCAN_BLOCK, LANES), F32),
        pltpu.VMEM((n_blocks, SCAN_BLOCK, LANES), F32),
        pltpu.VMEM((n_blocks, LANES, SCAN_BLOCK), F32),
        pltpu.VMEM((n_blocks, SCAN_BLOCK, 2 * LANES), BF16),
        pltpu.VMEM((n_blocks, SCAN_BLOCK, 2 * LANES), BF16),
        pltpu.VMEM((n_blocks, SCAN_BLOCK, 2 * LANES), BF16),
        pltpu.VMEM((n_blocks, 8, inner), F32),
    ]


def layer_forward(n_tensor, head_size, state, h, small, weights):
    tokens, width = h.shape
    inner = small["skip"].shape[1]
    n_blocks = tokens // SCAN_BLOCK
    groups = inner // GROUP
    operands = [h] + [
        small[name]
        for name in ("gain", "tap_x", "tap_b", "dt_bias", "aneg", "skip", "gate_gain", "live", "spread", "select")
    ]
    return pl.pallas_call(
        partial(forward_kernel, n_tensor, n_blocks, head_size),
        out_shape=[
            shaped((tokens, width)),
            shaped((PAD + tokens, width), BF16),
            shaped((tokens, inner)),
            shaped((PAD + tokens, inner)),
            shaped((PAD + tokens, 2 * state)),
            shaped((tokens, inner), BF16),
            shaped((tokens, 2 * state), BF16),
            shaped((tokens, LANES)),
            shaped((tokens, inner)),
            shaped((n_blocks + 1, state, inner)),
            shaped((tokens, LANES)),
        ],
        in_specs=[VMEM] * len(operands) + [ANY] * 4,
        out_specs=[VMEM] * 11,
        scratch_shapes=weight_scratch(width, inner, state, weights[2].shape[1])
        + [pltpu.VMEM((PAD, width), F32)]
        + block_scratch(n_blocks, inner)
        + [
            pltpu.VMEM((n_blocks, SCAN_BLOCK, SCAN_BLOCK), F32),
            pltpu.VMEM((n_blocks, state, inner), F32),
            pltpu.VMEM((groups, state, GROUP), BF16),
            pltpu.VMEM((groups, state, GROUP), BF16),
            pltpu.VMEM((tokens, inner), F32),
            pltpu.VMEM((tokens, inner), BF16),
            pltpu.VMEM((tokens, LANES), F32),
            pltpu.SemaphoreType.DMA((4,)),
            pltpu.SemaphoreType.DMA,
            pltpu.SemaphoreType.DMA,
            pltpu.SemaphoreType.DMA((groups,)),
            pltpu.SemaphoreType.DMA((groups,)),
        ],
        compiler_params=pltpu.CompilerParams(
            collective_id=1, has_side_effects=True, vmem_limit_bytes=60 * 1024 * 1024
        ),
        name="layer_forward",
    )(*operands, *weights)


def layer_backward(n_tensor, head_size, state, gh, h, small, saved, weights):
    tokens, width = h.shape
    inner = small["skip"].shape[1]
    n_blocks = tokens // SCAN_BLOCK
    groups = inner // GROUP
    operands = (
        [gh, h]
        + [
            small[name]
            for name in ("gain", "tap_x", "tap_b", "aneg", "skip", "gate_gain", "live", "spread", "select", "collect")
        ]
        + list(saved)
    )
    return pl.pallas_call(
        partial(backward_kernel, n_tensor, n_blocks, head_size),
        out_shape=[
            shaped((tokens, width)),
            shaped((width, inner), BF16),
            shaped((width, inner), BF16),
            shaped((width, inner), BF16),
            shaped((width, 2 * state + 2 * LANES), BF16),
            shaped((small_rows(width, inner, state)["all"], LANES)),
        ],
        in_specs=[VMEM] * len(operands) + [ANY] * 4,
        out_specs=[VMEM] * 6,
        scratch_shapes=weight_scratch(width, inner, state, weights[2].shape[1])
        + [
            pltpu.VMEM((tokens, width), BF16),
            pltpu.VMEM((width, tokens), BF16),
            pltpu.VMEM((width, tokens), BF16),
        ]
        + block_scratch(n_blocks, inner)
        + [
            pltpu.VMEM((n_blocks, SCAN_BLOCK, SCAN_BLOCK), F32),
            pltpu.VMEM((SCAN_BLOCK, SCAN_BLOCK), F32),
            pltpu.VMEM((tokens + PAD, inner), F32),
            pltpu.VMEM((tokens + PAD, 2 * state), F32),
            pltpu.VMEM((tokens, inner), BF16),
            pltpu.VMEM((tokens, inner), BF16),
            pltpu.VMEM((tokens, 2 * state), BF16),
            pltpu.VMEM((tokens, LANES), BF16),
            pltpu.VMEM((n_blocks, state, inner), F32),
            pltpu.VMEM((n_blocks + 1, state, inner), F32),
            pltpu.VMEM((groups, state, GROUP), BF16),
            pltpu.VMEM((groups, state, GROUP), BF16),
            pltpu.VMEM((8, LANES), F32),
            pltpu.VMEM((tokens, LANES), F32),
            pltpu.VMEM((SCAN_BLOCK, LANES), F32),
            pltpu.VMEM((SCAN_BLOCK, LANES), F32),
            pltpu.VMEM((SCAN_BLOCK, state), F32),
            pltpu.VMEM((SCAN_BLOCK, state), F32),
            pltpu.VMEM((tokens, width), F32),
            pltpu.VMEM((8, width), F32),
            pltpu.SemaphoreType.DMA((4,)),
            pltpu.SemaphoreType.DMA((2,)),
            pltpu.SemaphoreType.DMA((2,)),
            pltpu.SemaphoreType.DMA((groups,)),
            pltpu.SemaphoreType.DMA((groups,)),
        ],
        compiler_params=pltpu.CompilerParams(
            collective_id=2, has_side_effects=True, vmem_limit_bytes=60 * 1024 * 1024
        ),
        name="layer_backward",
    )(*operands, *weights)


def reduce_kernel(layers, part, state, *refs):
    n_units = 3 * (part // LANES) + 1
    wide = refs[: 4 * layers]
    small = refs[4 * layers]
    out_wide = refs[4 * layers + 1 : 4 * layers + 4]
    out_narrow, out_small = refs[4 * layers + 4 : 4 * layers + 6]
    total = layers * n_units
    rest = refs[4 * layers + 6 :]
    first, second, third, fourth = (rest[k * total : (k + 1) * total] for k in range(4))
    (small_core, small_x, small_y, small_z, sum_core, sum_x) = rest[4 * total : 4 * total + 6]
    sems = rest[4 * total + 6 :]
    send0, recv0, send1, recv1, send2, recv2, send3, recv3, send_n, recv_n, send_s, recv_s = sems

    n_dp, n_tensor = lax.axis_size("dp"), lax.axis_size("tensor")
    dp, tensor = lax.axis_index("dp"), lax.axis_index("tensor")
    core, x = lax.rem(tensor, 2), tensor // 2
    y, z = lax.rem(dp, 2), dp // 2
    depth = n_dp // 2
    rows = out_narrow.shape[2]
    to_core = {"tensor": tensor + 1 - 2 * core}
    to_x = {"tensor": lax.rem(tensor + 2, n_tensor)}
    to_y = {"dp": dp + 1 - 2 * y}
    to_z = [{"dp": lax.rem(z + k, depth) * 2 + y} for k in range(1, depth)]
    to_diagonal = {"tensor": n_tensor - 1 - tensor}

    barrier = pltpu.get_barrier_semaphore()
    partners = [to_core, to_x, to_diagonal, to_y] + to_z
    for partner in partners:
        pl.semaphore_signal(barrier, inc=1, device_id=partner, device_id_type=pl.DeviceIdType.MESH)
    pl.semaphore_wait(barrier, len(partners))

    def remote(source, target, send, recv, device):
        return pltpu.make_async_remote_copy(
            src_ref=source,
            dst_ref=target,
            send_sem=send,
            recv_sem=recv,
            device_id=device,
            device_id_type=pl.DeviceIdType.MESH,
        )

    units = []
    for layer in range(layers):
        for member in (2, 0, 1, 3):
            block = LANES if member == 3 else part
            for column in range(0, block, LANES):
                units.append((layer, member, block, column))

    def plan(index):
        layer, member, block, column = units[index]
        source = wide[4 * layer + member]
        r0, r1, r2, r3 = first[index], second[index], third[index], fourth[index]
        x_first = index % 2 == 0

        def lanes(side, which):
            return pl.ds(pl.multiple_of((2 * side + which) * block + column, LANES), LANES)

        copies0 = [
            remote(
                source.at[:, :, :, lanes(side, 1 - core)],
                r0.at[side],
                send0.at[index, side],
                recv0.at[index, side],
                to_core,
            )
            for side in range(2)
        ]
        if x_first:
            copy1 = remote(r0.at[1 - x], r1, send1.at[index], recv1.at[index], to_x)
            copy2 = remote(r1.at[:, 1 - y], r2, send2.at[index], recv2.at[index], to_y)
        else:
            copy1 = remote(r0.at[:, :, 1 - y], r1, send1.at[index], recv1.at[index], to_y)
            copy2 = remote(r1.at[1 - x], r2, send2.at[index], recv2.at[index], to_x)
        copies3 = [
            remote(
                r2.at[lax.rem(z + k, depth)],
                r3.at[k - 1],
                send3.at[index, k - 1],
                recv3.at[index, k - 1],
                to_z[k - 1],
            )
            for k in range(1, depth)
        ]

        def begin():
            for copy in copies0:
                copy.start()

        def after_core():
            for copy in copies0:
                copy.wait_recv()

            @pl.loop(0, 2 * depth)
            def _(step):
                high, low = step // 2, lax.rem(step, 2)
                for side in range(2):
                    r0[side, high, low] = (
                        r0[side, high, low].astype(F32)
                        + source[high, low, :, lanes(side, core)].astype(F32)
                    ).astype(BF16)

            copy1.start()

        def after_first():
            copy1.wait_recv()

            @pl.loop(0, depth)
            def _(high):
                for side in range(2):
                    if x_first:
                        r1[high, side] = (
                            r1[high, side].astype(F32) + r0[x, high, side].astype(F32)
                        ).astype(BF16)
                    else:
                        r1[side, high] = (
                            r1[side, high].astype(F32) + r0[side, high, y].astype(F32)
                        ).astype(BF16)

            copy2.start()

        def after_second():
            copy2.wait_recv()

            @pl.loop(0, depth)
            def _(high):
                mine = r1[high, y] if x_first else r1[x, high]
                r2[high] = (r2[high].astype(F32) + mine.astype(F32)).astype(BF16)

            for copy in copies3:
                copy.start()

        def finish():
            value = r2[z].astype(F32)
            for k, copy in enumerate(copies3):
                copy.wait_recv()
                value = value + r3[k].astype(F32)
            if member == 3:
                out_narrow[layer, tensor] = value
            else:
                out_wide[member][layer, :, column : column + LANES] = value

        def drain():
            for copy in copies0 + [copy1, copy2] + copies3:
                copy.wait_send()

        return begin, after_core, after_first, after_second, finish, drain

    plans = [plan(index) for index in range(total)]

    small_first = remote(small, small_core, send_s.at[0], recv_s.at[0], to_core)
    small_second = remote(sum_core, small_x, send_s.at[1], recv_s.at[1], to_x)
    small_third = remote(sum_x, small_y, send_s.at[2], recv_s.at[2], to_y)
    small_last = [
        remote(
            small_z.at[z], small_z.at[z], send_s.at[2 + k], recv_s.at[2 + k], to_z[k - 1]
        )
        for k in range(1, depth)
    ]

    def small_step(step):
        if step == 0:
            small_first.start()
        elif step == 1:
            small_first.wait_recv()
            sum_core[...] = small[...] + small_core[...]
            small_second.start()
        elif step == 2:
            small_second.wait_recv()
            sum_x[...] = sum_core[...] + small_x[...]
            small_third.start()
        elif step == 3:
            small_third.wait_recv()
            small_z[z] = sum_x[...] + small_y[...]
            for copy in small_last:
                copy.start()
        elif step == 4:
            for copy in small_last:
                copy.wait_recv()
            value = small_z[0]
            for k in range(1, depth):
                value = value + small_z[k]
            out_small[...] = value

    ahead = 2
    for index in range(min(ahead, total)):
        plans[index][0]()
    for step in range(total + 6):
        small_step(step)
        if step + ahead < total:
            plans[step + ahead][0]()
        for stage, delay in ((1, 0), (2, 2), (3, 4), (4, 6)):
            if 0 <= step - delay < total:
                plans[step - delay][stage]()

    narrow_copies = [
        remote(
            out_narrow.at[:, tensor],
            out_narrow.at[:, tensor],
            send_n.at[k - 1],
            recv_n.at[k - 1],
            {"tensor": lax.rem(tensor + k, n_tensor)},
        )
        for k in range(1, n_tensor)
    ]
    for copy in narrow_copies:
        copy.start()
    for copy in narrow_copies:
        copy.wait_recv()
    for entry in plans:
        entry[5]()
    for copy in [small_first, small_second, small_third] + small_last + narrow_copies:
        copy.wait_send()


def reduce_gradients(n_dp, n_tensor, part, state, wide, small):
    layers = len(wide)
    rows = wide[0][0].shape[0] // n_dp
    depth = n_dp // 2
    operands = [
        array.reshape(depth, 2, rows, array.shape[1]) for members in wide for array in members
    ] + [small]
    total = layers * (3 * (part // LANES) + 1)
    scratch = [pltpu.VMEM((2, depth, 2, rows, LANES), BF16)] * total
    for index in range(total):
        shape = (depth, 2, rows, LANES) if index % 2 == 0 else (2, depth, rows, LANES)
        scratch.append(pltpu.VMEM(shape, BF16))
    scratch += [pltpu.VMEM((depth, rows, LANES), BF16)] * total
    scratch += [pltpu.VMEM((depth - 1, rows, LANES), BF16)] * total
    scratch += [pltpu.VMEM(small.shape, F32)] * 3
    scratch += [pltpu.VMEM((depth,) + small.shape, F32)]
    scratch += [pltpu.VMEM(small.shape, F32)] * 2
    pairs = ((total, 2), (total,), (total,), (total, depth - 1), (n_tensor - 1,), (2 + depth,))
    for shape in pairs:
        scratch += [pltpu.SemaphoreType.DMA(shape)] * 2
    return pl.pallas_call(
        partial(reduce_kernel, layers, part, state),
        out_shape=[shaped((layers, rows, part))] * 3
        + [shaped((layers, n_tensor, rows, LANES)), shaped(small.shape)],
        in_specs=[VMEM] * len(operands),
        out_specs=[VMEM] * 5,
        scratch_shapes=scratch,
        compiler_params=pltpu.CompilerParams(
            collective_id=3, has_side_effects=True, vmem_limit_bytes=60 * 1024 * 1024
        ),
        name="reduce_gradients",
    )(*operands)


def gather_steps(n_dp, n_tensor, blocks, wholes, width, sems, x_first):
    send_z, recv_z, send_n, recv_n, own = sems
    dp, tensor = lax.axis_index("dp"), lax.axis_index("tensor")
    core, x = lax.rem(tensor, 2), tensor // 2
    y, z = lax.rem(dp, 2), dp // 2
    depth = n_dp // 2
    block, start, full = width
    to_core = {"tensor": tensor + 1 - 2 * core}
    to_x = {"tensor": lax.rem(tensor + 2, n_tensor)}
    to_y = {"dp": dp + 1 - 2 * y}

    def lanes(side):
        return pl.ds(pl.multiple_of((2 * side + core) * full + start, LANES), block)

    def remote(source, target, send, recv, device):
        return pltpu.make_async_remote_copy(
            src_ref=source,
            dst_ref=target,
            send_sem=send,
            recv_sem=recv,
            device_id=device,
            device_id_type=pl.DeviceIdType.MESH,
        )

    def same(place, slot, device):
        return remote(place, place, send_n.at[slot], recv_n.at[slot], device)

    mine = blocks.at[:, pl.ds(start, block)]
    keep = pltpu.make_async_copy(mine, wholes.at[z, y, :, lanes(x)], own)
    along_z = [
        remote(
            mine,
            wholes.at[z, y, :, lanes(x)],
            send_z.at[k - 1],
            recv_z.at[k - 1],
            {"dp": lax.rem(z + k, depth) * 2 + y},
        )
        for k in range(1, depth)
    ]
    if x_first:
        one = [same(wholes.at[:, y, :, lanes(x)], 0, to_x)]
        two = [same(wholes.at[:, y, :, lanes(side)], 1 + side, to_y) for side in range(2)]
    else:
        one = [same(wholes.at[:, y, :, lanes(x)], 0, to_y)]
        two = [same(wholes.at[:, :, :, lanes(x)], 1, to_x)]
    last = [same(wholes.at[:, :, :, lanes(side)], 3 + side, to_core) for side in range(2)]

    def begin():
        keep.start()
        for copy in along_z:
            copy.start()

    def hand_on(before, after):
        def step():
            for copy in before:
                copy.wait_recv()
            for copy in after:
                copy.start()

        return step

    def first():
        keep.wait()
        hand_on(along_z, one)()

    def finish():
        for copy in last:
            copy.wait_recv()
        for copy in along_z + one + two + last:
            copy.wait_send()

    return [begin, first, hand_on(one, two), hand_on(two, last), finish]


def gather_partners(n_dp, n_tensor):
    dp, tensor = lax.axis_index("dp"), lax.axis_index("tensor")
    core, y, z = lax.rem(tensor, 2), lax.rem(dp, 2), dp // 2
    depth = n_dp // 2
    return [
        {"tensor": tensor + 1 - 2 * core},
        {"tensor": lax.rem(tensor + 2, n_tensor)},
        {"dp": dp + 1 - 2 * y},
    ] + [{"dp": lax.rem(z + k, depth) * 2 + y} for k in range(1, depth)]


def gather_kernel(layers, part, *refs):
    arranged = refs[0]
    blocks = refs[1:5]
    hidden = refs[5]
    wholes = refs[6 : 6 + 4 * layers]
    send_z, recv_z, send_n, recv_n, own, deal_send, deal_recv, deal_own = refs[6 + 4 * layers :]
    n_dp, n_tensor = lax.axis_size("dp"), lax.axis_size("tensor")
    dp, tensor = lax.axis_index("dp"), lax.axis_index("tensor")
    parts = n_dp // n_tensor
    runner = dp // parts

    barrier = pltpu.get_barrier_semaphore()

    def greet(device):
        pl.semaphore_signal(barrier, inc=1, device_id=device, device_id_type=pl.DeviceIdType.MESH)

    partners = gather_partners(n_dp, n_tensor)
    for partner in partners:
        greet(partner)
    for k in range(parts):
        for other in range(n_tensor):
            source = tensor * parts + k

            @pl.when((source != dp) | (other != tensor))
            def _():
                greet({"dp": source, "tensor": other})

    with_self = (runner == tensor).astype(jnp.int32)
    pl.semaphore_wait(barrier, len(partners) + n_dp - with_self)

    deal_keep = pltpu.make_async_copy(
        arranged.at[dp], hidden.at[lax.rem(dp, parts), tensor], deal_own
    )
    deal = [
        pltpu.make_async_remote_copy(
            src_ref=arranged.at[j],
            dst_ref=hidden.at[lax.rem(dp, parts), tensor],
            send_sem=deal_send.at[j],
            recv_sem=deal_recv.at[lax.rem(dp, parts), tensor],
            device_id={"dp": j, "tensor": runner},
            device_id_type=pl.DeviceIdType.MESH,
        )
        for j in range(n_dp)
    ]
    for j in range(n_dp):
        remote_here = (j != dp) | (runner != tensor)

        @pl.when(remote_here)
        def _():
            deal[j].start()

    @pl.when(runner == tensor)
    def _():
        deal_keep.start()

    plans = []
    for layer in range(layers):
        for member in range(4):
            full = LANES if member == 2 else part
            for start in range(0, full, LANES):
                index = len(plans)
                plans.append(
                    gather_steps(
                        n_dp,
                        n_tensor,
                        blocks[member].at[layer],
                        wholes[4 * layer + member],
                        (LANES, start, full),
                        [sem.at[index] for sem in (send_z, recv_z, send_n, recv_n, own)],
                        index % 2 == 0,
                    )
                )
    total = len(plans)
    ahead = 3
    for index in range(min(ahead, total)):
        plans[index][0]()
    for step in range(total + 6):
        if step + ahead < total:
            plans[step + ahead][0]()
        for stage, delay in ((1, 0), (2, 2), (3, 4), (4, 6)):
            if 0 <= step - delay < total:
                plans[step - delay][stage]()

    for k in range(parts):
        for other in range(n_tensor):

            @pl.when((tensor * parts + k != dp) | (other != tensor))
            def _():
                pltpu.make_async_remote_copy(
                    src_ref=arranged.at[0],
                    dst_ref=hidden.at[k, other],
                    send_sem=deal_send.at[0],
                    recv_sem=deal_recv.at[k, other],
                    device_id={"dp": dp, "tensor": lax.rem(tensor + 1, n_tensor)},
                    device_id_type=pl.DeviceIdType.MESH,
                ).wait_recv()

    for j in range(n_dp):
        remote_here = (j != dp) | (runner != tensor)

        @pl.when(remote_here)
        def _():
            deal[j].wait_send()

    @pl.when(runner == tensor)
    def _():
        deal_keep.wait()


def gather_all(n_dp, n_tensor, arranged, blocks):
    layers, rows, part = blocks[0].shape
    piece, width = arranged.shape[1:]
    depth = n_dp // 2
    total = layers * (3 * (part // LANES) + 1)
    wholes = [
        shaped((depth, 2, rows, n_tensor * block.shape[2]), BF16)
        for layer in range(layers)
        for block in blocks
    ]
    results = pl.pallas_call(
        partial(gather_kernel, layers, part),
        out_shape=[shaped((n_dp // n_tensor, n_tensor, piece, width), BF16)] + wholes,
        in_specs=[ANY] * 5,
        out_specs=[ANY] * (1 + len(wholes)),
        scratch_shapes=[
            pltpu.SemaphoreType.DMA((total, depth - 1)),
            pltpu.SemaphoreType.DMA((total, depth - 1)),
            pltpu.SemaphoreType.DMA((total, 5)),
            pltpu.SemaphoreType.DMA((total, 5)),
            pltpu.SemaphoreType.DMA((total,)),
            pltpu.SemaphoreType.DMA((n_dp,)),
            pltpu.SemaphoreType.DMA((n_dp // n_tensor, n_tensor)),
            pltpu.SemaphoreType.DMA,
        ],
        compiler_params=pltpu.CompilerParams(collective_id=4, has_side_effects=True),
        name="gather_all",
    )(arranged, *blocks)
    tokens = n_dp * piece
    return results[0].reshape(tokens, width), [
        [whole.reshape(n_dp * rows, whole.shape[3]) for whole in results[1 + 4 * layer : 5 + 4 * layer]]
        for layer in range(layers)
    ]


def padded_lanes(values):
    return jnp.pad(values, ((0, 0), (0, LANES - values.shape[1])))


def padded_rows(values):
    return jnp.pad(values, ((0, 8 - values.shape[0]), (0, 0)))


def local(
    hidden_in,
    lengths,
    order,
    in_gain,
    w_z,
    w_x,
    w_bc,
    w_dt,
    conv_x,
    conv_bc,
    dt_bias,
    a_log,
    d_skip,
    gated_gain,
    w_out,
    cotangent,
):
    n_dp = lax.axis_size("dp")
    n_tensor = lax.axis_size("tensor")
    dp_index = lax.axis_index("dp")
    tensor_index = lax.axis_index("tensor")
    piece = hidden_in.shape[2]
    width = hidden_in.shape[3]
    tokens = piece * n_dp
    parts = n_dp // n_tensor
    layers = w_z.shape[0]
    inner = gated_gain.shape[1]
    heads = dt_bias.shape[1]
    head_size = inner // heads
    state = conv_bc.shape[2] // 2
    rows_local = w_z.shape[1]
    part = w_z.shape[2]

    def to_run(values):
        swapped = lax.all_to_all(
            values.reshape(n_tensor, parts, piece, width), "tensor", split_axis=0, concat_axis=0
        )
        return swapped.transpose(1, 0, 2, 3).reshape(tokens, width)

    def to_pieces(values):
        swapped = values.reshape(parts, n_tensor, piece, width).transpose(1, 0, 2, 3)
        return lax.all_to_all(swapped, "tensor", split_axis=0, concat_axis=0).reshape(
            n_dp, piece, width
        )

    seq_length = jnp.take(lengths, jnp.take(order, dp_index))
    arranged = jnp.take(hidden_in, order, axis=0)
    direct = rows_local % 16 == 0 and n_tensor == 4 and n_dp % 2 == 0
    quarter = 2 * state // n_tensor
    narrow = jnp.concatenate(
        [lax.dynamic_slice_in_dim(w_bc, tensor_index * quarter, quarter, 2), w_dt], axis=2
    )
    narrow = jnp.pad(narrow, ((0, 0), (0, 0), (0, LANES - narrow.shape[2])))
    blocks = (w_z, w_x, narrow, w_out)
    if direct:
        hidden, weights = gather_all(n_dp, n_tensor, arranged[:, 0], blocks)
    else:
        dealt = lax.all_to_all(arranged, "dp", split_axis=0, concat_axis=1, tiled=True)
        hidden = to_run(dealt[0])

        def whole(stacked):
            gathered = lax.all_gather(stacked, "dp", axis=1, tiled=True)
            return lax.all_gather(gathered, "tensor", axis=2, tiled=True)

        wholes = [whole(block) for block in blocks]
        weights = [[stacked[layer] for stacked in wholes] for layer in range(layers)]
    hidden = hidden.astype(F32)
    positions = tensor_index * tokens + jnp.arange(tokens)
    live = jnp.broadcast_to((positions < seq_length).astype(F32)[:, None], (tokens, LANES))

    head_ids = jnp.arange(inner) // head_size
    one_hot = (head_ids[:, None] == jnp.arange(LANES)[None, :]).astype(BF16)
    spread = jnp.concatenate([one_hot.T, one_hot.T], axis=0)
    source = jnp.arange(n_tensor * LANES)
    place = jnp.where(
        source % LANES < quarter,
        source // LANES * quarter + source % LANES,
        jnp.where(
            source % LANES < quarter + heads // n_tensor,
            2 * state + source // LANES * (heads // n_tensor) + source % LANES - quarter,
            -1,
        ),
    )
    select = (place[:, None] == jnp.arange(2 * state + LANES)[None, :]).astype(BF16)
    small = []
    for layer in range(layers):
        small.append(
            dict(
                gain=padded_rows(in_gain[layer][None]),
                tap_x=padded_rows(conv_x[layer]),
                tap_b=padded_rows(conv_bc[layer]),
                dt_bias=padded_rows(padded_lanes(dt_bias[layer][None])),
                aneg=padded_rows(padded_lanes(-jnp.exp(a_log[layer])[None])),
                skip=padded_rows(jnp.repeat(d_skip[layer], head_size)[None]),
                gate_gain=padded_rows(gated_gain[layer][None]),
                live=live,
                spread=spread,
                select=select,
                collect=one_hot,
            )
        )

    inputs, kept = [], []
    for layer in range(layers):
        inputs.append(hidden)
        results = layer_forward(n_tensor, head_size, state, hidden, small[layer], weights[layer])
        hidden = results[0]
        kept.append(results[1:])
    block_out = to_pieces(hidden.astype(BF16))[None]

    grad = to_run(cotangent[0]).astype(F32)
    wide_terms = [None] * layers
    small_terms = [None] * layers
    for layer in reversed(range(layers)):
        results = layer_backward(
            n_tensor, head_size, state, grad, inputs[layer], small[layer], kept[layer], weights[layer]
        )
        grad = results[0]
        wide_terms[layer] = results[1:5]
        small_terms[layer] = results[5]

    if direct:
        sum_z, sum_x, sum_out, sum_narrow, sum_small = reduce_gradients(
            n_dp, n_tensor, part, state, wide_terms, jnp.stack(small_terms)
        )
    else:

        def scattered(member):
            blocks = jnp.stack([terms[member] for terms in wide_terms]).astype(F32)
            mine = lax.psum_scatter(blocks, "dp", scatter_dimension=1, tiled=True)
            return lax.psum_scatter(mine, "tensor", scatter_dimension=2, tiled=True)

        sum_z, sum_x, sum_out, narrow = (scattered(member) for member in range(4))
        sum_narrow = lax.all_gather(narrow, "tensor", axis=1)
        sum_small = lax.psum(jnp.stack(small_terms), ("dp", "tensor"))
    sum_bc = jnp.concatenate([sum_narrow[:, 0], sum_narrow[:, 1]], axis=2)
    sum_dt = lax.dynamic_slice_in_dim(
        sum_narrow[:, 2], tensor_index * (heads // n_tensor), heads // n_tensor, 2
    )
    at = small_rows(width, inner, state)

    def taken(name, rows, shape):
        return sum_small[:, at[name] : at[name] + rows].reshape((layers,) + shape)

    returned = lax.all_to_all(
        to_pieces(grad.astype(BF16))[None], "dp", split_axis=1, concat_axis=0, tiled=True
    )
    input_grad = jnp.zeros_like(returned).at[order].set(returned)
    tap_rows = WIDTH + 1
    return (
        block_out,
        input_grad,
        taken("gain", width // LANES, (width,)),
        sum_z,
        sum_x,
        sum_bc,
        sum_dt,
        taken("tap_x", tap_rows * (inner // LANES), (tap_rows, inner)),
        taken("tap_b", tap_rows * (2 * state // LANES), (tap_rows, 2 * state)),
        sum_small[:, at["heads"], :heads],
        sum_small[:, at["heads"] + 1, :heads],
        sum_small[:, at["heads"] + 2, :heads],
        taken("gate_gain", inner // LANES, (inner,)),
        sum_out,
    )


def solution(mesh):
    return jax.shard_map(
        local,
        mesh=mesh,
        in_specs=(
            P(None, "dp", "tensor", None),
            P(),
            P(),
            P(),
            P(None, "dp", "tensor"),
            P(None, "dp", "tensor"),
            P(None, "dp", None),
            P(None, "dp", "tensor"),
            P(),
            P(),
            P(),
            P(),
            P(),
            P(),
            P(None, "dp", "tensor"),
            P("dp", None, "tensor", None),
        ),
        out_specs=(
            P("dp", None, "tensor", None),
            P(None, "dp", "tensor", None),
            P(),
            P(None, "dp", "tensor"),
            P(None, "dp", "tensor"),
            P(None, "dp", None),
            P(None, "dp", "tensor"),
            P(),
            P(),
            P(),
            P(),
            P(),
            P(),
            P(None, "dp", "tensor"),
        ),
        check_vma=False,
    )
```

time: 2020 us -> 504 us (0.25)
  waiting for transfers between devices: 633 us -> 11.7 us
  local copies, waits for them, and re-layouts: 588 us -> 36.3 us
  Pallas kernels: 0 us -> 403 us
  matrix products: 314 us -> 0 us
  other arithmetic: 320 us -> 13.7 us
  blocking collectives: 93.5 us -> 0 us
    pallas_call x0 -> x6, Pallas kernels: none -> 403 us  [the longest x2 128 us: layer_backward(): pl.pallas_call(partial(backward_kernel, n_tensor, n_blocks, head_size), o...]
    dynamic_update_slice x74 -> x0, local copies, waits for them, and re-layouts: 329 us -> none  [the longest x64 328 us: scan_product(): final_state, outputs = lax.scan(jax.checkpoint(advance), initial, pieces)]
    dot_general x210 -> x0, matrix products: 298 us -> none  [the longest x48 112 us: advance(): local_out = jnp.einsum('tsh,shp->thp', mixing, x_part, precision=HIGH)]
    another operation x182 -> x1, other arithmetic: 204 us -> 0.65 us  [local(): jnp.stack(small_terms)]
    psum x3 -> x0, waiting for transfers between devices: 179 us -> none  [the longest x1 106 us: local(): small_sums = lax.psum(small_stacks, ('dp', 'tensor'))]
    unnamed x19 -> x0, waiting for transfers between devices: 175 us -> none
    reduce_scatter x2 -> x0, waiting for transfers between devices: 136 us -> none  [local(): lax.psum_scatter(stacked_grads, 'dp', scatter_dimension=1, tiled=True)]
    all_gather x10 -> x0, waiting for transfers between devices: 78.8 us -> none  [the longest x2 41 us: local(): lax.all_gather(normed_piece, 'tensor', axis=1, tiled=True)]
  transfers between devices with their start and end apart: 23 -> 4, of which waited for: 15 -> 1; matrix products, arithmetic and copies ran while one was open for 43% -> 9% of each run, Pallas kernels for 0% -> 81%
where the time goes in v1:
time: 504 us; the launch traced here: 496 us
  Pallas kernels  403 us (80%)
  local copies, waits for them, and re-layouts  36.3 us (7%)
  starting transfers between devices  28.1 us (6%)
  other arithmetic  13.7 us (3%)
  waiting for transfers between devices  11.7 us (2%)
    pallas_call x2, Pallas kernels, layer_backward(): pl.pallas_call(partial(backward_kernel, n_tensor, n_blocks, head_size), o...  128 us
    pallas_call x1, Pallas kernels, gather_all(): pl.pallas_call(partial(gather_kernel, layers, part), out_shape=[shaped((n...  105 us
    pallas_call x1, Pallas kernels, reduce_gradients(): pl.pallas_call(partial(reduce_kernel, layers, part, state), out_shape=[sh...  102 us
    pallas_call x2, Pallas kernels, layer_forward(): pl.pallas_call(partial(forward_kernel, n_tensor, n_blocks, head_size), ou...  68.2 us
    all_to_all x2, starting transfers between devices, to_pieces(): lax.all_to_all(swapped, 'tensor', split_axis=0, concat_axis=0)  20.1 us
    all_to_all x2, waiting for transfers between devices, to_pieces(): lax.all_to_all(swapped, 'tensor', split_axis=0, concat_axis=0)  11.7 us
  transfers between devices with their start and end apart: 4, of which 1 were waited for; matrix products, arithmetic and copies ran while one was open for 9% of the time, Pallas kernels for 81%

profile of v1, /device:TPU:0, one launch (start us, length us, event | category | flops | bytes accessed | tf_op | source)
XLA Modules:
  0.0 495.7 jit_solution(6510769035969433632)
XLA Ops:
  0.7 4.4 all-to-all-start.1
  6.4 1.2 dynamic-slice.5
  9.9 1.0 fusion.26
  14.7 1.2 dynamic-slice.6
  17.6 1.0 broadcast_select_fusion.refs_0_
  29.0 104.6 %gather_all.1 = (bf16[2,4,64,768]{3,2,1,0:T(8,128)(2,1)}, bf16[4,2,96,1536]{3,2,1,0:T(8,128)(2,1)}, bf16[4,2,96,1536]{3,2,1,0:T(8,128)(2,1)}, bf16[4,2,96,512]{3...) custom-call(bf16[8,64,768]{2,1,0:T(8,128)(2,1)} %broadcast_select_fu, ...), custom_call_target="tpu_custom_call" | custom-call | tf_op jit(solution)/shard_map/gather_all/pallas_call | solution.py:1339
  133.6 0.9 add_convert_fusion.spread
  134.5 2.4 bitcast_convert_fusion.h
  137.8 33.8 %layer_forward.2 = (f32[512,768]{1,0:T(8,128)}, bf16[528,768]{1,0:T(8,128)(2,1)}, f32[512,1536]{1,0:T(8,128)}, f32[528,1536]{1,0:T(8,128)}, f32[528,256]{1,0:T(8...) custom-call(f32[512,768]{1,0:T(8,128)} %bitcast_convert_fusion.h, ...), custom_call_target="tpu_custom_call" | custom-call | tf_op jit(solution)/shard_map/layer_forward/pallas_call | solution.py:780
  171.6 34.4 %layer_forward.3 = (f32[512,768]{1,0:T(8,128)}, bf16[528,768]{1,0:T(8,128)(2,1)}, f32[512,1536]{1,0:T(8,128)}, f32[528,1536]{1,0:T(8,128)}, f32[528,256]{1,0:T(8...) custom-call(f32[512,768]{1,0:T(8,128)} %get-tuple-element.67.h, ...), custom_call_target="tpu_custom_call" | custom-call | tf_op jit(solution)/shard_map/layer_forward/pallas_call | solution.py:780
  206.0 1.5 convert_element_type.69
  208.5 15.9 %all-to-all-start = ((bf16[4,2,64,768]{3,2,1,0:T(8,128)(2,1)}), bf16[4,2,64,768]{3,2,1,0:T(8,128)(2,1)S(1)}, u32[]{:S(2)}, u32[]{:S(2)}) async-start(bf16[4,2,64,768]{3,2,1,0:T(8,128)(2,1)} %bitcast.71), calls=%async_computation | async-start | bytes 1572864 | tf_op jit(solution)/shard_map/all_to_all | solution.py:1414
  224.4 1.0 fusion.1.collect
  225.6 1.4 copy.59
  226.9 65.4 %layer_backward.2 = (f32[512,768]{1,0:T(8,128)}, bf16[768,1536]{1,0:T(8,128)(2,1)}, bf16[768,1536]{1,0:T(8,128)(2,1)}, bf16[768,1536]{1,0:T(8,128)(2,1)}, bf16[768,512]{1,0:T(8,128)(2,1)}, /*index=5*/f32[104,128]{1,0:T(8,128)}) custom-call(f32[512,768]{1,0:T(8,128)} %bitcast.91, f32[512,768]{1,0:T(8,128)} %get-tuple-element.67.h, f32[8,768]{1,0:T(8,128)} %pad.74.gain, ...), custom_call_target="tpu_custom_call" | custom-call | tf_op jit(solution)/shard_map/layer_backward/pallas_call | solution.py:834
  292.3 62.8 %layer_backward.3 = (f32[512,768]{1,0:T(8,128)}, bf16[768,1536]{1,0:T(8,128)(2,1)}, bf16[768,1536]{1,0:T(8,128)(2,1)}, bf16[768,1536]{1,0:T(8,128)(2,1)}, bf16[768,512]{1,0:T(8,128)(2,1)}, /*index=5*/f32[104,128]{1,0:T(8,128)}) custom-call(f32[512,768]{1,0:T(8,128)} %get-tuple-element.83.gh, f32[512,768]{1,0:T(8,128)} %bitcast_convert_fusion.h, ...), custom_call_target="tpu_custom_call" | custom-call | tf_op jit(solution)/shard_map/layer_backward/pallas_call | solution.py:834
  355.1 1.5 convert_element_type.74
  357.5 4.2 all-to-all-start.2
  361.7 11.7 %all-to-all-done.2 = bf16[4,2,64,768]{3,2,1,0:T(8,128)(2,1)} async-done(((bf16[4,2,64,768]{3,2,1,0:T(8,128)(2,1)}), bf16[4,2,64,768]{3,2,1,0:T(8,128)(2,1)}, u32[]{:S(2)}, u32[]{:S(2)}) %all-to-all-start.2) | async-done | bytes 786464 | tf_op jit(solution)/shard_map/all_to_all | solution.py:1414
  373.4 3.6 all-to-all-start.3
  377.7 102.2 %reduce_gradients.1 = (f32[2,96,384]{2,1,0:T(8,128)}, f32[2,96,384]{2,1,0:T(8,128)}, f32[2,96,384]{2,1,0:T(8,128)}, f32[2,4,96,128]{3,2,1,0:T(8,128)}, f32[2,104,128]{2,1,0:T(8,128)}) custom-call(bf16[4,2,96,1536]{3,2,1,0:T(8,128)(2,1)} %bitcast.104, bf16[4,2,96,1536]{3,2,1,0:T(8,128)(2,1)} %bitcast.105, bf16[4,2,96,1536]{3,2,1,0:T(8,128)(2,1)} %bitcast.106, ...), custom_call_target="tpu_custom_call" | custom-call | tf_op jit(solution)/shard_map/reduce_gradients/pallas_call | solution.py:1121
  482.9 1.0 fusion.24
  488.8 1.4 fusion.25
  492.1 1.7 copy.96
  (83 shorter events, 32.8 us)
Async XLA Ops:
  0.6 16.3 %copy-start = (bf16[8,1,64,768]{3,2,1,0:T(8,128)(2,1)S(1)}, bf16[8,1,64,768]{3,2,1,0:T(8,128)(2,1)}, u32[]{:S(2)}) copy-start(bf16[8,1,64,768]{3,2,1,0:T(8,128)(2,1)} %param.16) | copy-start | bytes 2359300
  0.7 207.8 %all-to-all-start.1 = ((bf16[4,2,64,768]{3,2,1,0:T(8,128)(2,1)}), bf16[4,2,64,768]{3,2,1,0:T(8,128)(2,1)S(1)}, u32[]{:S(2)}, u32[]{:S(2)}) async-start(bf16[4,2,64,768]{3,2,1,0:T(8,128)(2,1)} %bitcast.109), calls=%async_computation.1 | async-start | bytes 1572864 | tf_op jit(solution)/shard_map/all_to_all | solution.py:1407
  5.0 13.6 %copy-start.7 = (bf16[2,96,256]{2,1,0:T(8,128)(2,1)S(1)}, bf16[2,96,256]{2,1,0:T(8,128)(2,1)}, u32[]{:S(2)}) copy-start(bf16[2,96,256]{2,1,0:T(8,128)(2,1)} %param.22) | copy-start | bytes 294916
  208.5 149.0 %all-to-all-start = ((bf16[4,2,64,768]{3,2,1,0:T(8,128)(2,1)}), bf16[4,2,64,768]{3,2,1,0:T(8,128)(2,1)S(1)}, u32[]{:S(2)}, u32[]{:S(2)}) async-start(bf16[4,2,64,768]{3,2,1,0:T(8,128)(2,1)} %bitcast.71), calls=%async_computation | async-start | bytes 1572864 | tf_op jit(solution)/shard_map/all_to_all | solution.py:1414
  356.6 20.5 %copy-start.5 = (f32[104,128]{1,0:T(8,128)S(1)}, f32[104,128]{1,0:T(8,128)}, u32[]{:S(2)}) copy-start(f32[104,128]{1,0:T(8,128)} %get-tuple-element.104) | copy-start | bytes 159748
  356.6 20.5 %copy-start.6 = (f32[104,128]{1,0:T(8,128)S(1)}, f32[104,128]{1,0:T(8,128)}, u32[]{:S(2)}) copy-start(f32[104,128]{1,0:T(8,128)} %get-tuple-element.103) | copy-start | bytes 159748
  357.5 15.9 %all-to-all-start.2 = ((bf16[4,2,64,768]{3,2,1,0:T(8,128)(2,1)}), bf16[4,2,64,768]{3,2,1,0:T(8,128)(2,1)}, u32[]{:S(2)}, u32[]{:S(2)}) async-start(bf16[4,2,64,768]{3,2,1,0:T(8,128)(2,1)} %bitcast.70), calls=%async_computation.2 | async-start | bytes 1572864 | tf_op jit(solution)/shard_map/all_to_all | solution.py:1414
  373.4 116.8 %all-to-all-start.3 = ((bf16[1,8,64,768]{3,2,0,1:T(8,128)(2,1)}), bf16[1,8,64,768]{3,2,0,1:T(8,128)(2,1)S(1)}, u32[]{:S(2)}, u32[]{:S(2)}) async-start(bf16[1,8,64,768]{3,2,0,1:T(8,128)(2,1)} %bitcast.30), calls=%async_computation.3 | async-start | bytes 1572864 | tf_op jit(solution)/shard_map/all_to_all | solution.py:1517
  490.2 5.0 %copy-start.1 = (bf16[8,1,64,768]{3,2,1,0:T(8,128)(2,1)S(1)}, bf16[8,1,64,768]{3,2,1,0:T(8,128)(2,1)}, u32[]{:S(2)}) copy-start(bf16[8,1,64,768]{3,2,1,0:T(8,128)(2,1)} %param.16) | copy-start | bytes 2359300
  490.2 4.2 copy-start.3
  491.2 4.0 copy-start.2
  491.2 2.6 copy-start.4
